TPU v7x, 32 devices: a whole 2x2x4 slice. The times are simulated.
32 devices in a mesh: segment: 2 (over core), seq: 8 (over z, x), mp: 2 (over y).
Axes of the slice: x: 2, y: 2, z: 4, core: 2. Of those that a mesh axis runs over, the one named last changes fastest.
Arguments:
- inputs: bfloat16 [65536, 512], P('seq', 'mp'), may hold values from -6 to 6
- cotangent: bfloat16 [65536, 512], P('seq', 'mp'), may hold values from -0.375 to 0.375
- gate_gain: float32 [2, 512], P('segment', 'mp'), may hold values from 0.3 to 3
- key_gain: float32 [2, 512], P('segment', 'mp'), may hold values from 0.3 to 3
- first_factor: bfloat16 [2, 256, 256, 256], P('segment', 'seq'), may hold values from -0.375 to 0.375
- second_factor: bfloat16 [2, 256, 256, 256], P('segment', 'seq'), may hold values from -0.375 to 0.375
- up_first: bfloat16 [2, 4, 128, 128], P('segment', 'mp'), may hold values from -0.5 to 0.5
- up_second: bfloat16 [2, 4, 128, 512], P('segment', 'mp'), may hold values from -0.5 to 0.5
- down_first: bfloat16 [2, 4, 512, 128], P('segment', 'mp'), may hold values from -0.25 to 0.25
- down_second_weight: bfloat16 [2, 4, 128, 128], P('segment', 'mp'), may hold values from -0.5 to 0.5
Outputs:
- grad_first: float32 [2, 256, 256, 256], P('segment', 'seq', 'mp')
- grad_second: float32 [2, 256, 256, 256], P('segment', 'seq', 'mp')
All inputs are finite; a program needn't handle non-finite values.
Results may differ from a plain program's by a relative error of at most 0.024.
Values may be sent and summed in bfloat16 or wider, within the bound.
A program may use at most 192 MiB of HBM per device.

v0:
```python
import jax
import jax.numpy as jnp
from jax import lax
from jax.sharding import PartitionSpec as P


def sigmoid_slope(values):
    logistic = jax.nn.sigmoid(values)
    return logistic * (1.0 + values * (1.0 - logistic))


def reorder_dim(values, dim, outer, inner):
    shape = values.shape
    size = shape[dim]
    split = values.reshape(shape[:dim] + (outer, inner, size // (outer * inner)) + shape[dim + 1 :])
    return jnp.swapaxes(split, dim, dim + 1).reshape(shape)


def sequence_mix(scaled, first_block, second_block):
    mixed_rows = jnp.einsum(
        "aoi,aic->aoc", first_block, scaled, preferred_element_type=jnp.float32
    ).astype(jnp.bfloat16)
    columns = lax.all_to_all(
        mixed_rows, ("segment", "seq"), split_axis=1, concat_axis=0, tiled=True
    )
    turned_cols = jnp.einsum(
        "boi,ibc->obc", second_block, columns, preferred_element_type=jnp.float32
    ).astype(jnp.bfloat16)
    return (
        lax.all_to_all(turned_cols, ("segment", "seq"), split_axis=0, concat_axis=1, tiled=True),
        columns,
    )


def sequence_back(back_turned, mixed_cols, second_block):
    back_turned_cols = lax.all_to_all(
        back_turned, ("segment", "seq"), split_axis=1, concat_axis=0, tiled=True
    )
    second_grad = jnp.einsum(
        "obc,ibc->boi", back_turned_cols, mixed_cols, preferred_element_type=jnp.float32
    )
    back_mixed_cols = jnp.einsum(
        "boi,obc->ibc", second_block, back_turned_cols, preferred_element_type=jnp.float32
    ).astype(jnp.bfloat16)
    back_mixed = lax.all_to_all(
        back_mixed_cols, ("segment", "seq"), split_axis=0, concat_axis=1, tiled=True
    )
    return (back_mixed, second_grad)


def forward_pass(rows_in, weights, with_output):
    (
        gate_gain,
        key_gain,
        first_block,
        second_block,
        up_first,
        up_second,
        down_first,
        down_second_weight,
    ) = weights
    tokens = rows_in.shape[0]
    channels = rows_in.shape[1]
    row_blocks = first_block.shape[0]
    block_size = first_block.shape[1]
    local_blocks = up_first.shape[0]
    block_column_width = up_first.shape[1]
    total_blocks = local_blocks * lax.axis_size("mp")
    sub_width = block_column_width // total_blocks
    rows_grid = rows_in.reshape(row_blocks, block_size, channels).astype(jnp.float32)
    scaled = (rows_grid * key_gain).astype(jnp.bfloat16)
    turned, mixed_cols = sequence_mix(scaled, first_block, second_block)
    gate_pre = rows_grid * gate_gain
    hidden_rows = (rows_grid + jax.nn.silu(gate_pre) * turned.astype(jnp.float32)).astype(
        jnp.bfloat16
    )
    hidden_rows = hidden_rows.reshape(tokens, local_blocks, block_column_width)
    up_grid = up_first.reshape(local_blocks, block_column_width, total_blocks, sub_width)
    permuted = jnp.einsum(
        "tki,kijc->tjkc", hidden_rows, up_grid, preferred_element_type=jnp.float32
    ).astype(jnp.bfloat16)
    permuted = permuted.reshape(tokens, total_blocks, local_blocks * sub_width)
    gathered_in = lax.all_to_all(permuted, "mp", split_axis=1, concat_axis=2, tiled=True)
    preact = jnp.einsum("tjq,jqe->tje", gathered_in, up_second, preferred_element_type=jnp.float32)
    kept_state = (rows_grid, scaled, mixed_cols, turned, preact)
    if not with_output:
        return (None, kept_state)
    active = jax.nn.silu(preact).astype(jnp.bfloat16)
    down_grid = down_first.reshape(local_blocks, down_first.shape[1], total_blocks, sub_width)
    folded_rows = jnp.einsum(
        "tje,jemc->tmjc", active, down_grid, preferred_element_type=jnp.float32
    ).astype(jnp.bfloat16)
    folded_rows = folded_rows.reshape(tokens, total_blocks, local_blocks * sub_width)
    gathered_output = lax.all_to_all(folded_rows, "mp", split_axis=1, concat_axis=2, tiled=True)
    output_portion = jnp.einsum(
        "xds,dsl->xdl", gathered_output, down_second_weight, preferred_element_type=jnp.float32
    )
    result = (
        (hidden_rows.astype(jnp.float32) + output_portion)
        .reshape(tokens, channels)
        .astype(jnp.bfloat16)
    )
    return (result, kept_state)


def backward_pass(cot_rows, kept_state, weights):
    (
        gate_gain,
        key_gain,
        first_block,
        second_block,
        up_first,
        up_second,
        down_first,
        down_second_weight,
    ) = weights
    rows_grid, scaled, mixed_cols, turned, preact = kept_state
    tokens = cot_rows.shape[0]
    channels = cot_rows.shape[1]
    row_blocks = first_block.shape[0]
    block_size = first_block.shape[1]
    local_blocks = up_first.shape[0]
    block_column_width = up_first.shape[1]
    total_blocks = local_blocks * lax.axis_size("mp")
    sub_width = block_column_width // total_blocks
    up_grid = up_first.reshape(local_blocks, block_column_width, total_blocks, sub_width)
    down_grid = down_first.reshape(local_blocks, down_first.shape[1], total_blocks, sub_width)
    backward_folded_rows = jnp.einsum(
        "hsd,sad->hsa",
        cot_rows.reshape(tokens, local_blocks, block_column_width),
        down_second_weight,
        preferred_element_type=jnp.float32,
    ).astype(jnp.bfloat16)
    back_grid = lax.all_to_all(
        backward_folded_rows, "mp", split_axis=2, concat_axis=1, tiled=True
    ).reshape(tokens, total_blocks, local_blocks, sub_width)
    back_active = jnp.einsum(
        "tmjc,jemc->tje", back_grid, down_grid, preferred_element_type=jnp.float32
    )
    back_preact = (back_active * sigmoid_slope(preact)).astype(jnp.bfloat16)
    back_perm = jnp.einsum(
        "tje,jqe->tjq", back_preact, up_second, preferred_element_type=jnp.float32
    ).astype(jnp.bfloat16)
    back_perm_grid = lax.all_to_all(
        back_perm, "mp", split_axis=2, concat_axis=1, tiled=True
    ).reshape(tokens, total_blocks, local_blocks, sub_width)
    back_ffn = jnp.einsum(
        "tjkc,kijc->tki", back_perm_grid, up_grid, preferred_element_type=jnp.float32
    )
    back_hidden = cot_rows.astype(jnp.float32).reshape(
        row_blocks, block_size, channels
    ) + back_ffn.reshape(row_blocks, block_size, channels)
    gate_pre = rows_grid * gate_gain
    back_turned = (back_hidden * jax.nn.silu(gate_pre)).astype(jnp.bfloat16)
    back_mixed, second_grad = sequence_back(back_turned, mixed_cols, second_block)
    first_grad = jnp.einsum("aoc,aic->aoi", back_mixed, scaled, preferred_element_type=jnp.float32)
    back_scaled = jnp.einsum(
        "aoi,aoc->aic", first_block, back_mixed, preferred_element_type=jnp.float32
    )
    back_inputs = (
        back_hidden
        + back_hidden * turned.astype(jnp.float32) * sigmoid_slope(gate_pre) * gate_gain
        + back_scaled * key_gain
    )
    back_inputs = back_inputs.reshape(tokens, channels).astype(jnp.bfloat16)
    return (back_inputs, first_grad, second_grad)


def reduce_channels(first_grad, second_grad):
    totals_first, totals_second = (
        lax.psum(first_grad.astype(jnp.bfloat16), "mp").astype(jnp.float32),
        lax.psum(second_grad.astype(jnp.bfloat16), "mp").astype(jnp.float32),
    )
    half_rows = first_grad.shape[2] // lax.axis_size("mp")
    offset = lax.axis_index("mp") * half_rows
    share_first = lax.dynamic_slice_in_dim(totals_first, offset, half_rows, 2)
    share_second = lax.dynamic_slice_in_dim(totals_second, offset, half_rows, 2)
    return (share_first, share_second)


def on_device(
    inputs,
    cotangent,
    gate_gain,
    key_gain,
    first_factor,
    second_factor,
    up_first,
    up_second,
    down_first,
    down_second_weight,
):
    segment_count = lax.axis_size("segment")
    seq_count = lax.axis_size("seq")
    part_index = lax.axis_index("segment")
    gains_all = (
        lax.all_gather(gate_gain, "segment", axis=0, tiled=True),
        lax.all_gather(key_gain, "segment", axis=0, tiled=True),
    )
    blocks_all = (
        lax.all_gather(first_factor, "segment", axis=0, tiled=True),
        lax.all_gather(second_factor, "segment", axis=0, tiled=True),
        lax.all_gather(up_first, "segment", axis=0, tiled=True),
        lax.all_gather(up_second, "segment", axis=0, tiled=True),
        lax.all_gather(down_first, "segment", axis=0, tiled=True),
        lax.all_gather(down_second_weight, "segment", axis=0, tiled=True),
    )
    row_share = first_factor.shape[1] // segment_count
    local_rows = inputs.shape[0] // segment_count
    channels = inputs.shape[1]
    block_size = first_factor.shape[2]

    def layer_set(layer):
        first_block = lax.dynamic_slice_in_dim(
            blocks_all[0][layer], part_index * row_share, row_share, 0
        )
        second_block = lax.dynamic_slice_in_dim(
            blocks_all[1][layer], part_index * row_share, row_share, 0
        )
        first_block = reorder_dim(
            reorder_dim(first_block, 1, seq_count, segment_count), 2, seq_count, segment_count
        )
        second_block = reorder_dim(
            reorder_dim(second_block, 1, seq_count, segment_count), 2, seq_count, segment_count
        )
        return (
            gains_all[0][layer],
            gains_all[1][layer],
            first_block,
            second_block,
            blocks_all[2][layer],
            blocks_all[3][layer],
            blocks_all[4][layer],
            blocks_all[5][layer],
        )

    def local_order(rows):
        mine = lax.dynamic_slice_in_dim(rows, part_index * local_rows, local_rows, 0)
        grid = mine.reshape(local_rows // block_size, block_size, channels)
        return reorder_dim(grid, 1, seq_count, segment_count).reshape(local_rows, channels)

    lower = layer_set(0)
    upper = layer_set(1)
    middle, kept_lower = forward_pass(local_order(inputs), lower, True)
    unused_out, kept_upper = forward_pass(middle, upper, False)
    passed, first_upper, second_upper = backward_pass(local_order(cotangent), kept_upper, upper)
    ignored, first_lower, second_lower = backward_pass(passed, kept_lower, lower)
    first_both = jnp.stack([first_lower, first_upper])
    second_both = jnp.stack([second_lower, second_upper])
    first_both = reorder_dim(
        reorder_dim(first_both, 2, segment_count, seq_count), 3, segment_count, seq_count
    )
    second_both = reorder_dim(
        reorder_dim(second_both, 2, segment_count, seq_count), 3, segment_count, seq_count
    )
    share_first, share_second = reduce_channels(first_both, second_both)
    own_first, own_second = (
        lax.all_to_all(
            share_first.astype(jnp.bfloat16), "segment", split_axis=0, concat_axis=1, tiled=True
        ).astype(share_first.dtype),
        lax.all_to_all(
            share_second.astype(jnp.bfloat16), "segment", split_axis=0, concat_axis=1, tiled=True
        ).astype(share_second.dtype),
    )
    return (own_first, own_second)


def solution(mesh):
    placed = (
        P("seq", "mp"),
        P("seq", "mp"),
        P("segment", "mp"),
        P("segment", "mp"),
        P("segment", "seq", None, None),
        P("segment", "seq", None, None),
        P("segment", "mp", None, None),
        P("segment", "mp", None, None),
        P("segment", "mp", None, None),
        P("segment", "mp", None, None),
    )
    return jax.shard_map(
        on_device,
        mesh=mesh,
        in_specs=placed,
        out_specs=(P("segment", "seq", "mp", None), P("segment", "seq", "mp", None)),
        check_vma=False,
    )
```

profile of v0, /device:TPU:0, one launch (start us, length us, event | category | flops | bytes accessed | tf_op | source)
XLA Modules:
  0.0 1309.1 jit_solution(3061519233550325007)
XLA Ops:
  21.6 10.5 all-gather.5.cloned.1.call-done
  38.5 17.6 %copy.285 = bf16[16,2,8,16,256]{3,2,1,4,0:T(8,128)(2,1)} copy(bf16[16,2,8,16,256]{4,3,1,2,0:T(8,128)(2,1)} %bitcast.369) | data formatting | bytes 4194304 | tf_op jit(solution)/shard_map/transpose | solution.py:16
  56.1 20.6 %reshape_reshape.20 = bf16[16,256,8,2,16]{1,4,3,2,0:T(8,128)(2,1)} reshape(bf16[16,2,8,16,256]{3,2,1,4,0:T(8,128)(2,1)} %copy.285) | data formatting | bytes 4194304 | tf_op jit(solution)/shard_map/reshape;reshape | solution.py:15
  93.8 16.0 %copy.291 = bf16[16,2,8,16,256]{3,2,1,4,0:T(8,128)(2,1)} copy(bf16[16,2,8,16,256]{4,3,1,2,0:T(8,128)(2,1)S(1)} %bitcast.368) | data formatting | bytes 4194304 | tf_op jit(solution)/shard_map/transpose | solution.py:16
  109.8 20.6 %reshape_reshape.21 = bf16[16,256,8,2,16]{1,4,3,2,0:T(8,128)(2,1)} reshape(bf16[16,2,8,16,256]{3,2,1,4,0:T(8,128)(2,1)} %copy.291) | data formatting | bytes 4194304 | tf_op jit(solution)/shard_map/reshape;reshape | solution.py:15
  164.3 35.5 %all-to-all-done.2 = bf16[256,16,256]{2,1,0:T(8,128)(2,1)} async-done(((bf16[256,16,256]{2,1,0:T(8,128)(2,1)}), bf16[256,16,256]{2,1,0:T(8,128)(2,1)}, u32[]{:S(2)}, u32[]{:S(2)}) %all-to-all-start.2) | async-done | bytes 2097184 | tf_op jit(solution)/shard_map/all_to_all | solution.py:30
  227.4 19.7 %all-to-all-done.3 = bf16[4096,4,64]{0,2,1:T(8,128)(2,1)} async-done(((bf16[4096,4,64]{0,2,1:T(8,128)(2,1)}), bf16[4096,4,64]{0,2,1:T(8,128)(2,1)}, u32[]{:S(2)}, u32[]{:S(2)}) %all-to-all-start.3) | async-done | bytes 2097184 | tf_op jit(solution)/shard_map/all_to_all | solution.py:83
  265.7 17.5 %copy.307 = bf16[16,2,8,16,256]{3,2,1,4,0:T(8,128)(2,1)} copy(bf16[16,2,8,16,256]{4,3,1,2,0:T(8,128)(2,1)} %bitcast.363) | data formatting | bytes 4194304 | tf_op jit(solution)/shard_map/transpose | solution.py:16
  283.2 20.5 %reshape_reshape.22 = bf16[16,256,8,2,16]{1,4,3,2,0:T(8,128)(2,1)} reshape(bf16[16,2,8,16,256]{3,2,1,4,0:T(8,128)(2,1)} %copy.307) | data formatting | bytes 4194304 | tf_op jit(solution)/shard_map/reshape;reshape | solution.py:15
  311.8 16.1 %copy.386 = f32[4096,2,128]{2,1,0:T(2,128)} copy(f32[4096,2,128]{2,0,1:T(8,128)S(1)} %fusion.17) | data formatting | bytes 8388608 | tf_op jit(solution)/shard_map/convert_element_type | solution.py:70
  346.5 16.1 %copy.315 = bf16[16,2,8,16,256]{3,2,1,4,0:T(8,128)(2,1)} copy(bf16[16,2,8,16,256]{4,3,1,2,0:T(8,128)(2,1)S(1)} %bitcast.362) | data formatting | bytes 4194304 | tf_op jit(solution)/shard_map/transpose | solution.py:16
  362.5 20.5 %reshape_reshape.23 = bf16[16,256,8,2,16]{1,4,3,2,0:T(8,128)(2,1)} reshape(bf16[16,2,8,16,256]{3,2,1,4,0:T(8,128)(2,1)} %copy.315) | data formatting | bytes 4194304 | tf_op jit(solution)/shard_map/reshape;reshape | solution.py:15
  385.0 9.1 all-to-all-done.5
  427.5 30.5 %all-to-all-done.6 = bf16[256,16,256]{2,1,0:T(8,128)(2,1)} async-done(((bf16[256,16,256]{2,1,0:T(8,128)(2,1)}), bf16[256,16,256]{2,1,0:T(8,128)(2,1)}, u32[]{:S(2)}, u32[]{:S(2)}) %all-to-all-start.6) | async-done | bytes 2097184 | tf_op jit(solution)/shard_map/all_to_all | solution.py:30
  498.9 17.6 %all-to-all-done.7 = bf16[4096,4,64]{0,2,1:T(8,128)(2,1)} async-done(((bf16[4096,4,64]{0,2,1:T(8,128)(2,1)}), bf16[4096,4,64]{0,2,1:T(8,128)(2,1)}, u32[]{:S(2)}, u32[]{:S(2)}) %all-to-all-start.7) | async-done | bytes 2097184 | tf_op jit(solution)/shard_map/all_to_all | solution.py:83
  518.3 8.2 fusion.50
  526.5 12.9 fusion.20
  555.3 18.5 %all-to-all-done.8 = bf16[4096,2,128]{0,1,2:T(2,128)(2,1)} async-done(((bf16[4096,2,128]{0,1,2:T(2,128)(2,1)}), bf16[4096,2,128]{0,1,2:T(2,128)(2,1)}, u32[]{:S(2)}, u32[]{:S(2)}) %all-to-all-start.8) | async-done | bytes 2097184 | tf_op jit(solution)/shard_map/all_to_all | solution.py:144
  577.8 16.1 %copy.381 = f32[4096,2,128]{2,1,0:T(2,128)} copy(f32[4096,2,128]{2,0,1:T(8,128)S(1)} %convolution_bitcast_fusion.1) | data formatting | bytes 8388608 | tf_op jit(solution)/shard_map/reshape | solution.py:152
  600.5 8.5 bitcast_add_fusion
  610.2 57.5 %all_to_all.258 = bf16[16,256,256]{2,0,1:T(8,128)(2,1)S(1)} all-to-all(bf16[16,256,256]{2,0,1:T(8,128)(2,1)S(1)} %copy.334), channel_id=1, replica_groups=mesh['segment'=2,'seq'=8,'mp'=2] {'segment','seq'}, dimensions={1} | all-to-all | bytes 4194304 | tf_op jit(solution)/shard_map/all_to_all | solution.py:36
  677.4 53.4 %all_to_all.259 = bf16[256,16,256]{2,1,0:T(8,128)(2,1)S(1)} all-to-all(bf16[256,16,256]{2,1,0:T(8,128)(2,1)} %copy.339), channel_id=1, replica_groups=mesh['segment'=2,'seq'=8,'mp'=2] {'segment','seq'}, dimensions={0} | all-to-all | bytes 4194304 | tf_op jit(solution)/shard_map/all_to_all | solution.py:45
  753.0 24.1 %all-to-all-done.11 = bf16[4096,2,128]{0,1,2:T(2,128)(2,1)S(1)} async-done(((bf16[4096,2,128]{0,1,2:T(2,128)(2,1)}), bf16[4096,2,128]{0,1,2:T(2,128)(2,1)S(1)}, u32[]{:S(2)}, u32[]{:S(2)}) %all-to-all-start.11) | async-done | bytes 2097184 | tf_op jit(solution)/shard_map/all_to_all | solution.py:134
  778.6 12.6 fusion.21
  801.5 23.2 %all-to-all-done.12 = bf16[4096,2,128]{0,1,2:T(2,128)(2,1)S(1)} async-done(((bf16[4096,2,128]{0,1,2:T(2,128)(2,1)}), bf16[4096,2,128]{0,1,2:T(2,128)(2,1)S(1)}, u32[]{:S(2)}, u32[]{:S(2)}) %all-to-all-start.12) | async-done | bytes 2097184 | tf_op jit(solution)/shard_map/all_to_all | solution.py:144
  827.2 16.1 %copy.350 = f32[4096,2,128]{2,1,0:T(2,128)} copy(f32[4096,2,128]{2,0,1:T(8,128)S(1)} %convolution_bitcast_fusion) | data formatting | bytes 8388608 | tf_op jit(solution)/shard_map/tjkc,kijc->tki/transpose | solution.py:147
  855.8 54.3 %all_to_all.260 = bf16[16,256,256]{2,0,1:T(8,128)(2,1)S(1)} all-to-all(bf16[16,256,256]{2,0,1:T(8,128)(2,1)S(1)} %copy.351), channel_id=1, replica_groups=mesh['segment'=2,'seq'=8,'mp'=2] {'segment','seq'}, dimensions={1} | all-to-all | bytes 4194304 | tf_op jit(solution)/shard_map/all_to_all | solution.py:36
  930.9 33.3 %convert_element_type.326 = bf16[2,16,256,2,8,16]{5,4,3,2,1,0:T(8,128)(2,1)} reshape(bf16[2,16,8,2,16,256]{5,4,3,2,1,0:T(8,128)(2,1)} %copy_bitcast_fusion) | data formatting | bytes 8388608 | tf_op jit(solution)/shard_map/convert_element_type | solution.py:172
  964.2 34.9 %copy.367 = bf16[2,16,256,8,2,16]{2,5,4,3,1,0:T(8,128)(2,1)} copy(bf16[2,16,256,8,2,16]{5,3,4,2,1,0:T(8,128)(2,1)} %bitcast.325) | data formatting | bytes 8388608 | tf_op jit(solution)/shard_map/convert_element_type | solution.py:172
  1004.4 33.3 %convert_element_type.318 = bf16[2,16,256,2,8,16]{5,4,3,2,1,0:T(8,128)(2,1)} reshape(bf16[2,16,8,2,16,256]{5,4,3,2,1,0:T(8,128)(2,1)} %copy_bitcast_fusion.1) | data formatting | bytes 8388608 | tf_op jit(solution)/shard_map/convert_element_type | solution.py:171
  1037.7 34.9 %copy.360 = bf16[2,16,256,8,2,16]{2,5,4,3,1,0:T(8,128)(2,1)} copy(bf16[2,16,256,8,2,16]{5,3,4,2,1,0:T(8,128)(2,1)} %bitcast.326) | data formatting | bytes 8388608 | tf_op jit(solution)/shard_map/convert_element_type | solution.py:171
  1072.7 198.9 %all-reduce.3.cloned.1.call-done = (bf16[2,16,256,256]{2,3,1,0:T(8,128)(2,1)}, bf16[2,16,256,256]{2,3,1,0:T(8,128)(2,1)}) async-done(((bf16[2,16,256,256]{2,3,1,0:T(8,128)(2,1)}, bf16[2,16,256,256]{2,3,1,0:T(8,128)(2,1)}), (bf16[2,16,256,256]{2,3,1,0:T(8,128)(2,1)}, bf16[2,16,256,256]{2,3,1,0:T(8,128)(2,1)})) %all-reduce.3.cloned.1.call-update) | async-done | bytes 8388624 | tf_op jit(solution)/shard_map/psum | solution.py:171
  (198 shorter events, 365.0 us)
Async XLA Ops:
  7.2 25.0 %all-gather.5.cloned.1.call-start = ((), (), s32[]{:S(2)}) async-start(), calls=%async_computation.17 | async-start | bytes 12582912 | tf_op jit(solution)/shard_map/all_gather | solution.py:201
  7.9 80.2 %all-gather.7.cloned.1.call-start = ((), (), s32[]{:S(2)}) async-start(), calls=%async_computation.18 | async-start | bytes 12582912 | tf_op jit(solution)/shard_map/all_gather | solution.py:202
  21.6 56.9 %copy-start.2 = (bf16[16,256,256]{2,1,0:T(8,128)(2,1)}, bf16[16,256,256]{2,1,0:T(8,128)(2,1)S(1)}, u32[]{:S(2)}) copy-start(bf16[16,256,256]{2,1,0:T(8,128)(2,1)S(1)} %fusion.22) | copy-start | bytes 6291460
  81.9 53.8 %all-to-all-start.1 = ((bf16[16,256,256]{2,0,1:T(8,128)(2,1)}), bf16[16,256,256]{2,0,1:T(8,128)(2,1)}, u32[]{:S(2)}, u32[]{:S(2)}) async-start(bf16[16,256,256]{2,0,1:T(8,128)(2,1)} %copy.288), calls=%async_computation.1 | async-start | bytes 4194304 | tf_op jit(solution)/shard_map/all_to_all | solution.py:23
  132.2 6.0 copy-start.4
  146.9 5.3 copy-start.7
  146.9 52.9 %all-to-all-start.2 = ((bf16[256,16,256]{2,1,0:T(8,128)(2,1)}), bf16[256,16,256]{2,1,0:T(8,128)(2,1)}, u32[]{:S(2)}, u32[]{:S(2)}) async-start(bf16[256,16,256]{2,1,0:T(8,128)(2,1)} %copy.295), calls=%async_computation.2 | async-start | bytes 4194304 | tf_op jit(solution)/shard_map/all_to_all | solution.py:30
  154.8 5.8 copy-start.33
  154.8 7.6 copy-start.28
  164.3 309.0 %copy-start.24 = (bf16[2,2,128,128]{3,2,1,0:T(8,128)(2,1)}, bf16[2,2,128,128]{3,2,1,0:T(8,128)(2,1)S(1)}, u32[]{:S(2)}) copy-start(bf16[2,2,128,128]{3,2,1,0:T(8,128)(2,1)S(1)} %all_gather.30) | copy-start | bytes 393220
  164.3 46.2 %copy-start.30 = (f32[1,1,256]{2,1,0:T(1,128)}, f32[1,1,256]{2,1,0:T(1,128)S(1)}, u32[]{:S(2)}) copy-start(f32[1,1,256]{2,1,0:T(1,128)S(1)} %get-tuple-element.25) | copy-start | bytes 3076
  217.6 5.0 copy-start.26
  217.6 7.2 copy-start.27
  217.6 29.5 %all-to-all-start.3 = ((bf16[4096,4,64]{0,2,1:T(8,128)(2,1)}), bf16[4096,4,64]{0,2,1:T(8,128)(2,1)}, u32[]{:S(2)}, u32[]{:S(2)}) async-start(bf16[4096,4,64]{0,2,1:T(8,128)(2,1)} %bitcast.367), calls=%async_computation.3 | async-start | bytes 4194304 | tf_op jit(solution)/shard_map/all_to_all | solution.py:83
  251.3 5.8 copy-start.8
  258.8 5.0 copy-start.29
  258.8 48.1 %all-to-all-start.4 = ((bf16[4096,4,64]{0,2,1:T(8,128)(2,1)}), bf16[4096,4,64]{0,2,1:T(8,128)(2,1)}, u32[]{:S(2)}, u32[]{:S(2)}) async-start(bf16[4096,4,64]{0,2,1:T(8,128)(2,1)} %bitcast.366), calls=%async_computation.4 | async-start | bytes 4194304 | tf_op jit(solution)/shard_map/all_to_all | solution.py:94
  327.9 6.6 copy-start.15
  340.1 6.4 copy-start.23
  340.1 54.0 %all-to-all-start.5 = ((bf16[16,256,256]{2,0,1:T(8,128)(2,1)}), bf16[16,256,256]{2,0,1:T(8,128)(2,1)}, u32[]{:S(2)}, u32[]{:S(2)}) async-start(bf16[16,256,256]{2,0,1:T(8,128)(2,1)} %copy.312), calls=%async_computation.5 | async-start | bytes 4194304 | tf_op jit(solution)/shard_map/all_to_all | solution.py:23
  405.2 52.8 %all-to-all-start.6 = ((bf16[256,16,256]{2,1,0:T(8,128)(2,1)}), bf16[256,16,256]{2,1,0:T(8,128)(2,1)}, u32[]{:S(2)}, u32[]{:S(2)}) async-start(bf16[256,16,256]{2,1,0:T(8,128)(2,1)} %copy.319), calls=%async_computation.6 | async-start | bytes 4194304 | tf_op jit(solution)/shard_map/all_to_all | solution.py:30
  458.0 29.6 %all-to-all-start = ((bf16[4096,2,128]{0,1,2:T(2,128)(2,1)}), bf16[4096,2,128]{0,1,2:T(2,128)(2,1)}, u32[]{:S(2)}, u32[]{:S(2)}) async-start(bf16[4096,2,128]{0,1,2:T(2,128)(2,1)} %copy.278), calls=%async_computation | async-start | bytes 4194304 | tf_op jit(solution)/shard_map/all_to_all | solution.py:134
  487.6 28.9 %all-to-all-start.7 = ((bf16[4096,4,64]{0,2,1:T(8,128)(2,1)}), bf16[4096,4,64]{0,2,1:T(8,128)(2,1)}, u32[]{:S(2)}, u32[]{:S(2)}) async-start(bf16[4096,4,64]{0,2,1:T(8,128)(2,1)} %bitcast.365), calls=%async_computation.7 | async-start | bytes 4194304 | tf_op jit(solution)/shard_map/all_to_all | solution.py:83
  545.7 28.1 %all-to-all-start.8 = ((bf16[4096,2,128]{0,1,2:T(2,128)(2,1)}), bf16[4096,2,128]{0,1,2:T(2,128)(2,1)}, u32[]{:S(2)}, u32[]{:S(2)}) async-start(bf16[4096,2,128]{0,1,2:T(2,128)(2,1)} %copy.326), calls=%async_computation.8 | async-start | bytes 4194304 | tf_op jit(solution)/shard_map/all_to_all | solution.py:144
  672.7 59.6 %copy-start.16 = (bf16[16,256,2,8,16]{1,4,3,2,0:T(8,128)(2,1)S(1)}, bf16[16,256,2,8,16]{1,4,3,2,0:T(8,128)(2,1)}, u32[]{:S(2)}) copy-start(bf16[16,256,2,8,16]{1,4,3,2,0:T(8,128)(2,1)} %copy.308) | copy-start | bytes 6291460
  677.4 54.9 %copy-start.9 = (f32[16,16,16,256]{3,2,1,0:T(8,128)S(1)}, f32[16,16,16,256]{3,2,1,0:T(8,128)}, u32[]{:S(2)}) copy-start(f32[16,16,16,256]{3,2,1,0:T(8,128)} %copy.320) | copy-start | bytes 12582916
  749.1 28.0 %all-to-all-start.11 = ((bf16[4096,2,128]{0,1,2:T(2,128)(2,1)}), bf16[4096,2,128]{0,1,2:T(2,128)(2,1)S(1)}, u32[]{:S(2)}, u32[]{:S(2)}) async-start(bf16[4096,2,128]{0,1,2:T(2,128)(2,1)} %copy.342), calls=%async_computation.11 | async-start | bytes 4194304 | tf_op jit(solution)/shard_map/all_to_all | solution.py:134
  797.4 27.3 %all-to-all-start.12 = ((bf16[4096,2,128]{0,1,2:T(2,128)(2,1)}), bf16[4096,2,128]{0,1,2:T(2,128)(2,1)S(1)}, u32[]{:S(2)}, u32[]{:S(2)}) async-start(bf16[4096,2,128]{0,1,2:T(2,128)(2,1)} %copy.346), calls=%async_computation.12 | async-start | bytes 4194304 | tf_op jit(solution)/shard_map/all_to_all | solution.py:144
  843.3 6.6 copy-start.20
  843.3 6.6 copy-start.31
  916.9 82.2 %all-to-all-start.14 = ((bf16[256,16,256]{2,1,0:T(8,128)(2,1)}), bf16[256,16,256]{2,1,0:T(8,128)(2,1)}, u32[]{:S(2)}, u32[]{:S(2)}) async-start(bf16[256,16,256]{2,1,0:T(8,128)(2,1)} %copy.356), calls=%async_computation.14 | async-start | bytes 4194304 | tf_op jit(solution)/shard_map/all_to_all | solution.py:45
  921.5 350.1 %all-reduce.3.cloned.1.call-start = ((), (), s32[]{:S(2)}) async-start(), calls=%async_computation.19 | async-start | bytes 16777216 | tf_op jit(solution)/shard_map/psum | solution.py:171
  (17 other events, 39.3 us)
Sparse Core Ops, SparseCore 0:
  9.5 22.5 all-gather.4
  33.7 21.0 all-gather.6
  1072.8 198.7 all-reduce.2
where the time goes:
time: 1320 us; the launch traced here: 1310 us
  local copies, waits for them, and re-layouts  522 us (40%)
  waiting for transfers between devices  400 us (30%)
  blocking collectives  188 us (14%)
  matrix products  81.1 us (6%)
  starting transfers between devices  60.5 us (5%)
  other arithmetic  41.9 us (3%)
  between operations  14.8 us (1%)
    psum x1, waiting for transfers between devices, reduce_channels(): lax.psum(first_grad.astype(jnp.bfloat16), 'mp').astype(jnp.float32)  199 us
    all_to_all x2, blocking collectives, sequence_back(): lax.all_to_all(back_turned, ('segment', 'seq'), split_axis=1, concat_axis...  112 us
    another operation x4, local copies, waits for them, and re-layouts, reorder_dim(): values.reshape(shape[:dim] + (outer, inner, size // (outer * inner)) + sh...  82.2 us
    transpose x9, local copies, waits for them, and re-layouts, reorder_dim(): return jnp.swapaxes(split, dim, dim + 1).reshape(shape)  79.3 us
    convert_element_type x2, local copies, waits for them, and re-layouts, reduce_channels(): second_grad.astype(jnp.bfloat16)  68.2 us
    convert_element_type x2, local copies, waits for them, and re-layouts, reduce_channels(): first_grad.astype(jnp.bfloat16)  68.2 us
    all_to_all x2, waiting for transfers between devices, sequence_mix(): lax.all_to_all(turned_cols, ('segment', 'seq'), split_axis=0, concat_axis...  66 us
    all_to_all x1, blocking collectives, sequence_back(): lax.all_to_all(back_mixed_cols, ('segment', 'seq'), split_axis=0, concat_...  53.4 us
  transfers between devices with their start and end apart: 15, of which 12 were waited for; matrix products, arithmetic and copies ran while one was open for 24% of the time, Pallas kernels for 0%

commit v1 on v0

v1 whole, which is shorter than its diff:
```python
import functools

import jax
import jax.numpy as jnp
from jax import lax
from jax.experimental import pallas as pl
from jax.experimental.pallas import tpu as pltpu
from jax.sharding import PartitionSpec as P

ALL = ("seq", "segment", "mp")
VMEM_LIMIT = 48 * 1024 * 1024
BF = jnp.bfloat16
F32 = jnp.float32


def logistic(values):
    return 0.5 + 0.5 * jnp.tanh(0.5 * values)


def dot(left, right):
    return lax.dot_general(left, right, (((1,), (0,)), ((), ())), preferred_element_type=F32)


def dot_nt(left, right):
    return lax.dot_general(left, right, (((1,), (1,)), ((), ())), preferred_element_type=F32)


def dot_tn(left, right):
    return lax.dot_general(left, right, (((0,), (0,)), ((), ())), preferred_element_type=F32)


def rows_kernel(x_ref, key_ref, first_ref, mixed_ref):
    scaled = (x_ref[0].astype(F32) * key_ref[...]).astype(BF)
    mixed_ref[0] = dot(first_ref[0], scaled).astype(BF)


def rows_back_kernel(bm_ref, x_ref, key_ref, first_ref, grad_ref, scaled_ref):
    back = bm_ref[0]
    scaled = (x_ref[0].astype(F32) * key_ref[...]).astype(BF)
    grad_ref[0] = dot_nt(back, scaled).astype(BF)
    scaled_ref[0] = dot_tn(first_ref[0], back).astype(BF)


def rows_grad_kernel(bm_ref, x_ref, key_ref, grad_ref):
    scaled = (x_ref[0].astype(F32) * key_ref[...]).astype(BF)
    grad_ref[0] = dot_nt(bm_ref[0], scaled).astype(BF)


def gate_part(mixed, second, x, gate):
    turned = dot(second, mixed).astype(BF).astype(F32)
    gate_pre = x * gate
    sig = logistic(gate_pre)
    hidden = (x + gate_pre * sig * turned).astype(BF)
    return turned, gate_pre, sig, hidden


def forward_kernel(mixed_ref, second_ref, x_ref, gate_ref, up1, up2, down1, down2, out_ref):
    width = up2.shape[1]
    x = x_ref[0].astype(F32)
    _, _, _, hidden = gate_part(mixed_ref[0], second_ref[0], x, gate_ref[...])
    permuted = dot(hidden, up1[...]).astype(BF)
    folded = []
    for j in range(up2.shape[0]):
        pre = dot(permuted[:, j * width : (j + 1) * width], up2[j])
        active = (pre * logistic(pre)).astype(BF)
        folded.append(dot(active, down1[j]).astype(BF))
    folded = jnp.concatenate(folded, axis=1)
    out_ref[0] = (hidden.astype(F32) + dot(folded, down2[...])).astype(BF)


def backward_body(cot, mixed, second, x, gate, up1, up2, down1, down2):
    width = up2.shape[1]
    turned, gate_pre, sig, hidden = gate_part(mixed, second, x, gate)
    permuted = dot(hidden, up1[...]).astype(BF)
    back_fold = dot_nt(cot, down2[...]).astype(BF)
    back_perm = []
    for j in range(up2.shape[0]):
        cols = slice(j * width, (j + 1) * width)
        pre = dot(permuted[:, cols], up2[j])
        back_active = dot_nt(back_fold[:, cols], down1[j])
        act_sig = logistic(pre)
        back_pre = (back_active * (act_sig * (1.0 + pre * (1.0 - act_sig)))).astype(BF)
        back_perm.append(dot_nt(back_pre, up2[j]).astype(BF))
    back_perm = jnp.concatenate(back_perm, axis=1)
    back_hidden = cot.astype(F32) + dot_nt(back_perm, up1[...])
    back_turned = (back_hidden * (gate_pre * sig)).astype(BF)
    second_grad = dot_nt(back_turned, mixed).astype(BF)
    back_mixed = dot_tn(second, back_turned).astype(BF)
    direct = back_hidden + back_hidden * turned * (sig * (1.0 + gate_pre * (1.0 - sig))) * gate
    return second_grad, back_mixed, direct


def upper_kernel(
    cot_ref, mixed_ref, second_ref, x_ref, gate_ref, up1, up2, down1, down2,
    grad_ref, back_ref, direct_ref,
):
    x = x_ref[0].astype(F32)
    grad_ref[0], back_ref[0], direct_ref[0] = backward_body(
        cot_ref[0], mixed_ref[0], second_ref[0], x, gate_ref[...], up1, up2, down1, down2
    )


def lower_kernel(
    direct_ref, scaled_ref, key_ref, mixed_ref, second_ref, x_ref, gate_ref,
    up1, up2, down1, down2, grad_ref, back_ref,
):
    x = x_ref[0].astype(F32)
    cot = (direct_ref[0] + scaled_ref[0].astype(F32) * key_ref[...]).astype(BF)
    grad_ref[0], back_ref[0], _ = backward_body(
        cot, mixed_ref[0], second_ref[0], x, gate_ref[...], up1, up2, down1, down2
    )


def blocked(shape):
    return pl.BlockSpec((1,) + tuple(shape[1:]), lambda n: (n,) + (0,) * (len(shape) - 1))


def whole(shape):
    return pl.BlockSpec(tuple(shape), lambda n: (0,) * len(shape))


def run(kernel, steps, operands, outs, flops):
    moved = sum(a.size * a.dtype.itemsize for a, _ in operands)
    moved += sum(int(jnp.dtype(d).itemsize) * functools.reduce(lambda p, q: p * q, s) for s, d in outs)
    result = pl.pallas_call(
        kernel,
        grid=(steps,),
        in_specs=[(blocked if cut else whole)(a.shape) for a, cut in operands],
        out_specs=[blocked(s) for s, _ in outs],
        out_shape=[jax.ShapeDtypeStruct(s, d) for s, d in outs],
        cost_estimate=pl.CostEstimate(flops=flops, bytes_accessed=moved, transcendentals=0),
        compiler_params=pltpu.CompilerParams(
            vmem_limit_bytes=VMEM_LIMIT, dimension_semantics=("arbitrary",)
        ),
    )(*[a for a, _ in operands])
    return result


def turn(rows):
    own, full, channels = rows.shape
    count = lax.axis_size(ALL)
    sent = jnp.swapaxes(rows, 0, 1)
    got = lax.all_to_all(sent, ALL, split_axis=0, concat_axis=0, tiled=True)
    got = got.reshape(count, full // count, own, channels)
    return jnp.swapaxes(got, 0, 1).reshape(full // count, count * own, channels)


def turn_split(rows):
    own, full, channels = rows.shape
    count = lax.axis_size(ALL)
    parts = lax.axis_size("mp")
    sent = jnp.swapaxes(rows, 0, 1)
    got = lax.all_to_all(sent, ALL, split_axis=0, concat_axis=0, tiled=True)
    got = got.reshape(count // parts, parts, full // count, own, channels)
    return jnp.transpose(got, (2, 0, 3, 1, 4)).reshape(
        full // count, count // parts * own, parts * channels
    )


def spread_pair(first, last):
    layers, blocks, width, _ = first.shape
    sub = width // blocks
    row = lax.broadcasted_iota(jnp.int32, (blocks, width, blocks * width), 1)
    col = lax.broadcasted_iota(jnp.int32, (blocks, width, blocks * width), 2)
    block = lax.broadcasted_iota(jnp.int32, (blocks, width, blocks * width), 0)
    place = (row // sub) * width + block * sub + row % sub
    spread = (col == place).astype(BF)
    up = jnp.einsum("lkir,krn->lkin", first, spread, preferred_element_type=F32)
    down = jnp.einsum("krn,lkrf->lnkf", spread, last, preferred_element_type=F32)
    full = blocks * width
    return up.astype(BF).reshape(layers, full, full), down.astype(BF).reshape(layers, full, full)


def on_device(
    inputs, cotangent, gate_gain, key_gain, first_factor, second_factor,
    up_first, up_second, down_first, down_second_weight,
):
    segments = lax.axis_size("segment")
    parts = lax.axis_size("mp")
    segment = lax.axis_index("segment")
    part = lax.axis_index("mp")
    size = first_factor.shape[2]
    held = first_factor.shape[1]
    channels = inputs.shape[1]
    model = channels * parts
    core_rows = held // segments
    own = core_rows // parts

    gains = jnp.concatenate([key_gain, gate_gain], axis=0)
    gains = lax.all_gather(gains, ("segment", "mp"), axis=0, tiled=False)
    gains = jnp.transpose(gains.reshape(segments, parts, 2, channels), (2, 0, 1, 3))
    gains = gains.reshape(2, segments, 1, model)
    keys, gates = gains[0], gains[1]

    first_all = lax.all_to_all(
        first_factor.reshape(segments, core_rows, size, size), "segment",
        split_axis=0, concat_axis=0, tiled=True,
    )
    first_low = first_all[0]
    first_high = lax.dynamic_slice_in_dim(first_all[1], part * own, own, 0)
    second_mine = lax.dynamic_index_in_dim(
        second_factor.reshape(segments, parts, own, size, size), part, 1, keepdims=False
    )
    second_all = lax.all_to_all(second_mine, "segment", split_axis=0, concat_axis=0, tiled=True)

    core_in = lax.dynamic_slice_in_dim(
        inputs.reshape(held, size, channels), segment * core_rows, core_rows, 0
    )
    core_cot = lax.dynamic_slice_in_dim(
        cotangent.reshape(held, size, channels), segment * core_rows, core_rows, 0
    )

    blocks = up_first.shape[1]
    width = up_first.shape[2]
    packed = jnp.concatenate(
        [
            a.reshape(blocks, -1, width)
            for a in (up_first[0], up_second[0], down_first[0], down_second_weight[0])
        ],
        axis=1,
    )
    packed = lax.all_gather(packed, ("segment", "mp"), axis=0, tiled=False)
    packed = packed.reshape(segments, parts * blocks, -1, width)
    hidden = up_second.shape[3]
    cuts = (0, width, width + hidden, width + 2 * hidden, 2 * width + 2 * hidden)
    piece = [packed[:, :, cuts[n] : cuts[n + 1]] for n in range(4)]
    ups = piece[1].reshape(segments, parts * blocks, width, hidden)
    downs = piece[2]
    wide_up, wide_down = spread_pair(piece[0], piece[3])

    def ffn(layer):
        return [
            (wide_up[layer], False), (ups[layer], False),
            (downs[layer], False), (wide_down[layer], False),
        ]

    grid_rows = (own, size, model)
    grad_shape = (own, size, size)
    cube = 2 * own * size * size * model
    feed = 2 * own * size * model * (2 * model + 2 * hidden)

    key_low = lax.dynamic_slice_in_dim(keys[0], part * channels, channels, 1)
    (mixed_low,) = run(
        rows_kernel, core_rows,
        [(core_in, True), (key_low, False), (first_low, True)],
        [((core_rows, size, channels), BF)], cube,
    )
    mixed_low = turn_split(mixed_low)
    in_cols = turn_split(core_in)
    (middle,) = run(
        forward_kernel, own,
        [(mixed_low, True), (second_all[0], True), (in_cols, True), (gates[0], False)] + ffn(0),
        [(grid_rows, BF)], cube + feed,
    )
    middle_rows = turn(middle)
    (mixed_high,) = run(
        rows_kernel, own,
        [(middle_rows, True), (keys[1], False), (first_high, True)],
        [(grid_rows, BF)], cube,
    )
    mixed_high = turn(mixed_high)
    cot_cols = turn_split(core_cot)
    second_high, back_high, direct = run(
        upper_kernel, own,
        [
            (cot_cols, True), (mixed_high, True), (second_all[1], True),
            (middle, True), (gates[1], False),
        ] + ffn(1),
        [(grad_shape, BF), (grid_rows, BF), (grid_rows, F32)], 3 * cube + 2 * feed,
    )
    back_rows = turn(back_high)
    grad_high, back_scaled = run(
        rows_back_kernel, own,
        [(back_rows, True), (middle_rows, True), (keys[1], False), (first_high, True)],
        [(grad_shape, BF), (grid_rows, BF)], 2 * cube,
    )
    scaled_cols = turn(back_scaled)
    second_low, back_low = run(
        lower_kernel, own,
        [
            (direct, True), (scaled_cols, True), (keys[1], False), (mixed_low, True),
            (second_all[0], True), (in_cols, True), (gates[0], False),
        ] + ffn(0),
        [(grad_shape, BF), (grid_rows, BF)], 3 * cube + 2 * feed,
    )
    in_rows = lax.all_to_all(core_in, "mp", split_axis=0, concat_axis=2, tiled=True)
    low_rows = turn(back_low)
    (grad_low,) = run(
        rows_grad_kernel, own,
        [(low_rows, True), (in_rows, True), (keys[0], False)],
        [(grad_shape, BF)], cube,
    )

    def hand_out(low, high):
        both = jnp.stack([low, high]).reshape(segments, own, parts, size // parts, size)
        both = jnp.swapaxes(both, 1, 2).reshape(segments * parts, own, size // parts, size)
        got = lax.all_to_all(both, ("segment", "mp"), split_axis=0, concat_axis=0, tiled=True)
        return got.reshape(1, held, size // parts, size).astype(F32)

    return hand_out(grad_low, grad_high), hand_out(second_low, second_high)


def solution(mesh):
    placed = (
        P("seq", "mp"),
        P("seq", "mp"),
        P("segment", "mp"),
        P("segment", "mp"),
        P("segment", "seq", None, None),
        P("segment", "seq", None, None),
        P("segment", "mp", None, None),
        P("segment", "mp", None, None),
        P("segment", "mp", None, None),
        P("segment", "mp", None, None),
    )
    return jax.shard_map(
        on_device,
        mesh=mesh,
        in_specs=placed,
        out_specs=(P("segment", "seq", "mp", None), P("segment", "seq", "mp", None)),
        check_vma=False,
    )
```

time: 1320 us -> 652 us (0.49)
  local copies, waits for them, and re-layouts: 522 us -> 103 us
  waiting for transfers between devices: 400 us -> 275 us
  matrix products: 81.1 us -> 1.22 us
  Pallas kernels: 0 us -> 74.4 us
  blocking collectives: 188 us -> 114 us
  other arithmetic: 41.9 us -> 10.8 us
    convert_element_type x29 -> x0, local copies, waits for them, and re-layouts: 244 us -> none  [the longest x2 68.2 us: reduce_channels(): second_grad.astype(jnp.bfloat16)]
    psum x1 -> x0, waiting for transfers between devices: 199 us -> none  [reduce_channels(): lax.psum(first_grad.astype(jnp.bfloat16), 'mp').astype(jnp.float32)]
    another operation x5 -> x1, local copies, waits for them, and re-layouts: 86.2 us -> 0.16 us  [on_device(): a.reshape(blocks, -1, width)]
    all_to_all x12 -> x11, waiting for transfers between devices: 189 us -> 275 us  [the longest x3 127 us: turn(): got = lax.all_to_all(sent, ALL, split_axis=0, concat_axis=0, tiled=True)]
    pallas_call x0 -> x7, Pallas kernels: none -> 74.4 us  [run(): pl.pallas_call(kernel, grid=(steps,), in_specs=[(blocked if cut else whol...]
    all_to_all x5 -> x2, blocking collectives: 176 us -> 104 us  [turn(): got = lax.all_to_all(sent, ALL, split_axis=0, concat_axis=0, tiled=True)]
    dot_general x20 -> x2, matrix products: 70 us -> 1.22 us  [the longest x1 0.62 us: spread_pair(): jnp.einsum('krn,lkrf->lnkf', spread, last, preferred_element_type=F32)]
    transpose x10 -> x11, local copies, waits for them, and re-layouts: 95.4 us -> 30.1 us  [the longest x5 12.9 us: turn(): sent = jnp.swapaxes(rows, 0, 1)]
  transfers between devices with their start and end apart: 15 -> 12, of which waited for: 12 -> 8; matrix products, arithmetic and copies ran while one was open for 24% -> 12% of each run, Pallas kernels for 0% -> 5%
where the time goes in v1:
time: 652 us; the launch traced here: 641 us
  waiting for transfers between devices  275 us (42%)
  blocking collectives  114 us (17%)
  local copies, waits for them, and re-layouts  103 us (16%)
  Pallas kernels  74.4 us (11%)
  starting transfers between devices  48.4 us (7%)
  between operations  15.1 us (2%)
  other arithmetic  10.8 us (2%)
    all_to_all x3, waiting for transfers between devices, turn(): got = lax.all_to_all(sent, ALL, split_axis=0, concat_axis=0, tiled=True)  127 us
    all_to_all x3, waiting for transfers between devices, turn_split(): got = lax.all_to_all(sent, ALL, split_axis=0, concat_axis=0, tiled=True)  114 us
    all_to_all x2, blocking collectives, turn(): got = lax.all_to_all(sent, ALL, split_axis=0, concat_axis=0, tiled=True)  104 us
    pallas_call x7, Pallas kernels, run(): pl.pallas_call(kernel, grid=(steps,), in_specs=[(blocked if cut else whol...  74.4 us
    all_to_all x2, waiting for transfers between devices, hand_out(): lax.all_to_all(both, ('segment', 'mp'), split_axis=0, concat_axis=0, tile...  33.4 us
    all_to_all x3, starting transfers between devices, turn_split(): got = lax.all_to_all(sent, ALL, split_axis=0, concat_axis=0, tiled=True)  14.2 us
    reshape x3, local copies, waits for them, and re-layouts, turn_split(): jnp.transpose(got, (2, 0, 3, 1, 4))  13.2 us
  transfers between devices with their start and end apart: 12, of which 8 were waited for; matrix products, arithmetic and copies ran while one was open for 12% of the time, Pallas kernels for 5%

profile of v1, /device:TPU:0, one launch (start us, length us, event | category | flops | bytes accessed | tf_op | source)
XLA Modules:
  0.0 641.0 jit_solution(1674311355837996869)
XLA Ops:
  7.2 5.7 all-to-all-start.1
  13.0 9.1 %all-gather.2 = f32[4,2,256]{2,1,0:T(2,128)S(1)} all-gather(f32[1,2,256]{2,1,0:T(2,128)S(1)} %maximum_bitcast_fusion), channel_id=2, replica_groups=mesh['segment'=2,'seq'=8,'mp'=2] {'segment','mp'}, dimensions={0}, use_global_device_ids=true | all-gather | bytes 10240 | tf_op jit(solution)/shard_map/all_gather | solution.py:190
  30.7 4.7 fusion.11
  35.4 9.7 %shard_map.113 = bf16[16,256,256]{2,1,0:T(8,128)(2,1)S(1)} custom-call(bf16[16,256,256]{2,1,0:T(8,128)(2,1)} %constant_dynamic-slice_fusion.1.x_ref, f32[1,256]{1,0:T(1,128)S(1)} %constant_dynamic-slice_fusion.key_ref, bf16[16,256,256]{2,1,0:T(8,128)(2,1)} %get-tuple-element.17.first_ref), custom_call_target="tpu_custom_call" | custom-call | flops 536870912 | bytes 6292480 | tf_op jit(solution)/shard_map/pallas_call | solution.py:125
  49.1 6.6 %all-to-all-start.2 = ((bf16[256,16,256]{2,1,0:T(8,128)(2,1)}), bf16[256,16,256]{2,1,0:T(8,128)(2,1)S(1)}, u32[]{:S(2)}, u32[]{:S(2)}) async-start(bf16[256,16,256]{2,1,0:T(8,128)(2,1)} %copy.60), calls=%async_computation.2 | async-start | bytes 4194304 | tf_op jit(solution)/shard_map/all_to_all | solution.py:153
  61.1 43.3 %all-to-all-done.2 = bf16[256,16,256]{2,1,0:T(8,128)(2,1)S(1)} async-done(((bf16[256,16,256]{2,1,0:T(8,128)(2,1)}), bf16[256,16,256]{2,1,0:T(8,128)(2,1)S(1)}, u32[]{:S(2)}, u32[]{:S(2)}) %all-to-all-start.2) | async-done | bytes 2097184 | tf_op jit(solution)/shard_map/all_to_all | solution.py:153
  105.8 4.0 all-to-all-start.4
  120.9 4.6 copy.110
  125.4 4.4 reshape.144.mixed_ref
  129.8 28.6 %all-to-all-done.4 = bf16[256,16,256]{2,1,0:T(8,128)(2,1)} async-done(((bf16[256,16,256]{2,1,0:T(8,128)(2,1)}), bf16[256,16,256]{2,1,0:T(8,128)(2,1)}, u32[]{:S(2)}, u32[]{:S(2)}) %all-to-all-start.4) | async-done | bytes 2097184 | tf_op jit(solution)/shard_map/all_to_all | solution.py:153
  158.4 6.1 copy.109
  164.6 4.4 reshape.147.x_ref
  169.0 14.4 %shard_map.114.x_ref = bf16[8,256,512]{2,1,0:T(8,128)(2,1)S(1)} custom-call(bf16[8,256,512]{2,1,0:T(8,128)(2,1)} %reshape.144.mixed_ref, bf16[8,256,256]{2,1,0:T(8,128)(2,1)S(1)} %get-tuple-element.25.second_ref, bf16[8,256,512]{2,1,0:T(8,128)(2,1)} %reshape.147.x_ref, f32[1,512]{1,0:T(1,128)S(1)} %bitcast.158, bf16[512,512]{1,0:T(8,128)(2,1)S(1)} %bitcast.150, ...), custom_call_target="tpu_custom_call" | custom-call | flops 4831838208 | bytes 9439232 | tf_op jit(solution)/shard_map/pallas_call | solution.py:125
  195.2 44.5 %all-to-all-done.5 = bf16[256,8,512]{2,1,0:T(8,128)(2,1)S(1)} async-done(((bf16[256,8,512]{2,1,0:T(8,128)(2,1)}), bf16[256,8,512]{2,1,0:T(8,128)(2,1)S(1)}, u32[]{:S(2)}, u32[]{:S(2)}) %all-to-all-start.5) | async-done | bytes 2097184 | tf_op jit(solution)/shard_map/all_to_all | solution.py:143
  251.2 42.1 %all-to-all-done = bf16[256,16,256]{2,1,0:T(8,128)(2,1)S(1)} async-done(((bf16[256,16,256]{2,1,0:T(8,128)(2,1)}), bf16[256,16,256]{2,1,0:T(8,128)(2,1)S(1)}, u32[]{:S(2)}, u32[]{:S(2)}) %all-to-all-start) | async-done | bytes 2097184 | tf_op jit(solution)/shard_map/all_to_all | solution.py:153
  301.1 6.1 copy.58
  307.2 4.4 reshape.139.cot_ref
  311.6 35.5 %all-to-all-done.6 = bf16[256,8,512]{2,1,0:T(8,128)(2,1)} async-done(((bf16[256,8,512]{2,1,0:T(8,128)(2,1)}), bf16[256,8,512]{2,1,0:T(8,128)(2,1)}, u32[]{:S(2)}, u32[]{:S(2)}) %all-to-all-start.6) | async-done | bytes 2097184 | tf_op jit(solution)/shard_map/all_to_all | solution.py:143
  350.4 20.2 %shard_map.116 = (bf16[8,256,256]{2,1,0:T(8,128)(2,1)S(1)}, bf16[8,256,512]{2,1,0:T(8,128)(2,1)}, f32[8,256,512]{2,1,0:T(8,128)}) custom-call(bf16[8,256,512]{2,1,0:T(8,128)(2,1)} %reshape.139.cot_ref, bf16[8,256,512]{2,1,0:T(8,128)(2,1)} %bitcast.178, bf16[8,256,256]{2,1,0:T(8,128)(2,1)S(1)} %copy-done.6, bf16[8,256,512]{2,1,0:T(8,128)(2,1)} %copy-done.3, ...), custom_call_target="tpu_custom_call" | custom-call | flops 10200547328 | bytes 16779264 | tf_op jit(solution)/shard_map/pallas_call | solution.py:125
  373.3 52.2 %all_to_all.78 = bf16[256,8,512]{2,1,0:T(8,128)(2,1)S(1)} all-to-all(bf16[256,8,512]{2,1,0:T(8,128)(2,1)S(1)} %copy.73), channel_id=1, replica_groups=mesh['segment'=2,'seq'=8,'mp'=2] {'seq','segment','mp'}, dimensions={0} | all-to-all | bytes 4194304 | tf_op jit(solution)/shard_map/all_to_all | solution.py:143
  427.0 5.9 shard_map.117
  434.1 52.3 %all_to_all.79 = bf16[256,8,512]{2,1,0:T(8,128)(2,1)} all-to-all(bf16[256,8,512]{2,1,0:T(8,128)(2,1)S(1)} %copy.75), channel_id=1, replica_groups=mesh['segment'=2,'seq'=8,'mp'=2] {'seq','segment','mp'}, dimensions={0} | all-to-all | bytes 4194304 | tf_op jit(solution)/shard_map/all_to_all | solution.py:143
  486.4 4.8 all-to-all-start.10
  494.6 20.0 %shard_map.118 = (bf16[8,256,256]{2,1,0:T(8,128)(2,1)S(1)}, bf16[8,256,512]{2,1,0:T(8,128)(2,1)}) custom-call(f32[8,256,512]{2,1,0:T(8,128)} %get-tuple-element.9.direct_ref, bf16[8,256,512]{2,1,0:T(8,128)(2,1)} %bitcast.179, f32[1,512]{1,0:T(1,128)S(1)} %bitcast.155, bf16[8,256,512]{2,1,0:T(8,128)(2,1)} %reshape.144.mixed_ref, ...), custom_call_target="tpu_custom_call" | custom-call | flops 10200547328 | bytes 16781312 | tf_op jit(solution)/shard_map/pallas_call | solution.py:125
  514.6 4.1 copy.77
  518.7 4.3 all-to-all-start.9
  524.6 47.1 %all-to-all-done.9 = bf16[256,8,512]{2,1,0:T(8,128)(2,1)} async-done(((bf16[256,8,512]{2,1,0:T(8,128)(2,1)}), bf16[256,8,512]{2,1,0:T(8,128)(2,1)}, u32[]{:S(2)}, u32[]{:S(2)}) %all-to-all-start.9) | async-done | bytes 2097184 | tf_op jit(solution)/shard_map/all_to_all | solution.py:143
  571.7 4.5 all-to-all-start.12
  576.1 5.1 copy.103
  590.0 11.9 %all-to-all-done.12 = bf16[4,8,128,256]{3,2,1,0:T(8,128)(2,1)} async-done(((bf16[4,8,128,256]{3,2,1,0:T(8,128)(2,1)}), bf16[4,8,128,256]{3,2,1,0:T(8,128)(2,1)}, u32[]{:S(2)}, u32[]{:S(2)}) %all-to-all-start.12) | async-done | bytes 2097184 | tf_op jit(solution)/shard_map/all_to_all | solution.py:297
  605.5 4.1 bitcast_convert_fusion
  609.6 21.5 %all-to-all-done.11 = bf16[4,8,128,256]{3,2,1,0:T(8,128)(2,1)S(1)} async-done(((bf16[4,8,128,256]{3,2,1,0:T(8,128)(2,1)}), bf16[4,8,128,256]{3,2,1,0:T(8,128)(2,1)S(1)}, u32[]{:S(2)}, u32[]{:S(2)}) %all-to-all-start.11) | async-done | bytes 2097184 | tf_op jit(solution)/shard_map/all_to_all | solution.py:297
  (121 shorter events, 89.7 us)
Async XLA Ops:
  7.2 5.8 copy-start.28
  7.2 5.8 copy-start.29
  7.2 19.8 %all-to-all-start.1 = ((bf16[2,16,256,256]{3,2,1,0:T(8,128)(2,1)}), bf16[2,16,256,256]{3,2,1,0:T(8,128)(2,1)}, u32[]{:S(2)}, u32[]{:S(2)}) async-start(bf16[2,16,256,256]{3,2,1,0:T(8,128)(2,1)} %bitcast.173), calls=%async_computation.1 | async-start | bytes 8388608 | tf_op jit(solution)/shard_map/all_to_all | solution.py:195
  22.1 3.3 copy-start.23
  26.9 20.7 %all-to-all-start.3 = ((bf16[2,8,256,256]{3,2,1,0:T(8,128)(2,1)}), bf16[2,8,256,256]{3,2,1,0:T(8,128)(2,1)S(1)}, u32[]{:S(2)}, u32[]{:S(2)}) async-start(bf16[2,8,256,256]{3,2,1,0:T(8,128)(2,1)} %dynamic-slice_bitcast_fusion), calls=%async_computation.3 | async-start | bytes 4194304 | tf_op jit(solution)/shard_map/all_to_all | solution.py:204
  47.6 8.1 %copy-start.25 = (bf16[1,2,128,512]{3,2,1,0:T(8,128)(2,1)S(1)}, bf16[1,2,128,512]{3,2,1,0:T(8,128)(2,1)}, u32[]{:S(2)}) copy-start(bf16[1,2,128,512]{3,2,1,0:T(8,128)(2,1)} %param.17) | copy-start | bytes 786436
  47.6 8.3 %copy-start.24 = (bf16[1,2,512,128]{3,2,1,0:T(8,128)(2,1)S(1)}, bf16[1,2,512,128]{3,2,1,0:T(8,128)(2,1)}, u32[]{:S(2)}) copy-start(bf16[1,2,512,128]{3,2,1,0:T(8,128)(2,1)} %param.18) | copy-start | bytes 786436
  47.6 8.3 %copy-start.26 = (bf16[1,2,128,128]{3,2,1,0:T(8,128)(2,1)S(1)}, bf16[1,2,128,128]{3,2,1,0:T(8,128)(2,1)}, u32[]{:S(2)}) copy-start(bf16[1,2,128,128]{3,2,1,0:T(8,128)(2,1)} %param.19) | copy-start | bytes 196612
  47.6 8.3 %copy-start.27 = (bf16[1,2,128,128]{3,2,1,0:T(8,128)(2,1)S(1)}, bf16[1,2,128,128]{3,2,1,0:T(8,128)(2,1)}, u32[]{:S(2)}) copy-start(bf16[1,2,128,128]{3,2,1,0:T(8,128)(2,1)} %param.16) | copy-start | bytes 196612
  49.1 55.4 %all-to-all-start.2 = ((bf16[256,16,256]{2,1,0:T(8,128)(2,1)}), bf16[256,16,256]{2,1,0:T(8,128)(2,1)S(1)}, u32[]{:S(2)}, u32[]{:S(2)}) async-start(bf16[256,16,256]{2,1,0:T(8,128)(2,1)} %copy.60), calls=%async_computation.2 | async-start | bytes 4194304 | tf_op jit(solution)/shard_map/all_to_all | solution.py:153
  55.7 56.8 %all-gather.5.cloned.1.call-start = ((), (), s32[]{:S(2)}) async-start(), calls=%async_computation.13 | async-start | bytes 3276800 | tf_op jit(solution)/shard_map/all_gather | solution.py:222
  105.8 52.6 %all-to-all-start.4 = ((bf16[256,16,256]{2,1,0:T(8,128)(2,1)}), bf16[256,16,256]{2,1,0:T(8,128)(2,1)}, u32[]{:S(2)}, u32[]{:S(2)}) async-start(bf16[256,16,256]{2,1,0:T(8,128)(2,1)} %copy.63), calls=%async_computation.4 | async-start | bytes 4194304 | tf_op jit(solution)/shard_map/all_to_all | solution.py:153
  112.5 56.5 %copy-start.4 = (bf16[8,256,256]{2,1,0:T(8,128)(2,1)}, bf16[8,256,256]{2,1,0:T(8,128)(2,1)S(1)}, u32[]{:S(2)}) copy-start(bf16[8,256,256]{2,1,0:T(8,128)(2,1)S(1)} %get-tuple-element.25.second_ref) | copy-start | bytes 3145732
  115.6 53.4 %copy-start.14 = (bf16[4,512,128]{2,1,0:T(8,128)(2,1)}, bf16[4,512,128]{2,1,0:T(8,128)(2,1)S(1)}, u32[]{:S(2)}) copy-start(bf16[4,512,128]{2,1,0:T(8,128)(2,1)S(1)} %get-tuple-element.20.down1) | copy-start | bytes 1572868
  115.9 53.1 %copy-start.7 = (bf16[4,128,512]{2,1,0:T(8,128)(2,1)}, bf16[4,128,512]{2,1,0:T(8,128)(2,1)S(1)}, u32[]{:S(2)}) copy-start(bf16[4,128,512]{2,1,0:T(8,128)(2,1)S(1)} %squeeze.79.up2) | copy-start | bytes 1572868
  118.9 50.1 %copy-start.9 = (bf16[512,512]{1,0:T(8,128)(2,1)}, bf16[512,512]{1,0:T(8,128)(2,1)S(1)}, u32[]{:S(2)}) copy-start(bf16[512,512]{1,0:T(8,128)(2,1)S(1)} %copy.83.down2) | copy-start | bytes 1572868
  120.4 48.6 %copy-start.11 = (bf16[1,4,128,512]{3,2,0,1:T(8,128)(2,1)}, bf16[1,4,128,512]{3,2,0,1:T(8,128)(2,1)S(1)}, u32[]{:S(2)}) copy-start(bf16[1,4,128,512]{3,2,0,1:T(8,128)(2,1)S(1)} %get-tuple-element.29) | copy-start | bytes 1572868
  187.3 52.4 %all-to-all-start.5 = ((bf16[256,8,512]{2,1,0:T(8,128)(2,1)}), bf16[256,8,512]{2,1,0:T(8,128)(2,1)S(1)}, u32[]{:S(2)}, u32[]{:S(2)}) async-start(bf16[256,8,512]{2,1,0:T(8,128)(2,1)} %copy.68), calls=%async_computation.5 | async-start | bytes 4194304 | tf_op jit(solution)/shard_map/all_to_all | solution.py:143
  241.0 52.4 %all-to-all-start = ((bf16[256,16,256]{2,1,0:T(8,128)(2,1)}), bf16[256,16,256]{2,1,0:T(8,128)(2,1)S(1)}, u32[]{:S(2)}, u32[]{:S(2)}) async-start(bf16[256,16,256]{2,1,0:T(8,128)(2,1)} %copy.57), calls=%async_computation | async-start | bytes 4194304 | tf_op jit(solution)/shard_map/all_to_all | solution.py:153
  294.7 52.5 %all-to-all-start.6 = ((bf16[256,8,512]{2,1,0:T(8,128)(2,1)}), bf16[256,8,512]{2,1,0:T(8,128)(2,1)}, u32[]{:S(2)}, u32[]{:S(2)}) async-start(bf16[256,8,512]{2,1,0:T(8,128)(2,1)} %copy.70), calls=%async_computation.6 | async-start | bytes 4194304 | tf_op jit(solution)/shard_map/all_to_all | solution.py:143
  347.1 3.3 copy-start.6
  347.1 3.3 copy-start.13
  347.1 3.3 copy-start.16
  486.4 32.2 %all-to-all-start.10 = ((bf16[16,256,256]{2,1,0:T(8,128)(2,1)}), bf16[16,256,256]{2,1,0:T(8,128)(2,1)}, u32[]{:S(2)}, u32[]{:S(2)}) async-start(bf16[16,256,256]{2,1,0:T(8,128)(2,1)} %constant_dynamic-slice_fusion.1.x_ref), calls=%async_computation.10 | async-start | bytes 4194304 | tf_op jit(solution)/shard_map/all_to_all | solution.py:286
  491.3 3.3 copy-start.5
  491.3 3.3 copy-start.8
  491.3 3.3 copy-start.10
  491.3 3.3 copy-start.12
  491.3 3.3 copy-start.15
  518.7 53.0 %all-to-all-start.9 = ((bf16[256,8,512]{2,1,0:T(8,128)(2,1)}), bf16[256,8,512]{2,1,0:T(8,128)(2,1)}, u32[]{:S(2)}, u32[]{:S(2)}) async-start(bf16[256,8,512]{2,1,0:T(8,128)(2,1)} %copy.77), calls=%async_computation.9 | async-start | bytes 4194304 | tf_op jit(solution)/shard_map/all_to_all | solution.py:143
  571.7 30.2 %all-to-all-start.12 = ((bf16[4,8,128,256]{3,2,1,0:T(8,128)(2,1)}), bf16[4,8,128,256]{3,2,1,0:T(8,128)(2,1)}, u32[]{:S(2)}, u32[]{:S(2)}) async-start(bf16[4,8,128,256]{3,2,1,0:T(8,128)(2,1)} %bitcast.166), calls=%async_computation.12 | async-start | bytes 4194304 | tf_op jit(solution)/shard_map/all_to_all | solution.py:297
  601.9 29.3 %all-to-all-start.11 = ((bf16[4,8,128,256]{3,2,1,0:T(8,128)(2,1)}), bf16[4,8,128,256]{3,2,1,0:T(8,128)(2,1)S(1)}, u32[]{:S(2)}, u32[]{:S(2)}) async-start(bf16[4,8,128,256]{3,2,1,0:T(8,128)(2,1)} %bitcast.167), calls=%async_computation.11 | async-start | bytes 4194304 | tf_op jit(solution)/shard_map/all_to_all | solution.py:297
  (10 other events, 16.0 us)
Sparse Core Ops, SparseCore 0:
  58.1 35.6 all-gather.4

commit v2 on v1

--- a/solution.py
+++ b/solution.py
@@ -29,6 +29,15 @@
     return lax.dot_general(left, right, (((0,), (0,)), ((), ())), preferred_element_type=F32)
 
 
+def column(ref):
+    if len(ref.shape) == 3:
+        return ref[0]
+    senders, parts, _, own, channels = ref.shape
+    return jnp.concatenate(
+        [ref[:, n, 0].reshape(senders * own, channels) for n in range(parts)], axis=1
+    )
+
+
 def rows_kernel(x_ref, key_ref, first_ref, mixed_ref):
     scaled = (x_ref[0].astype(F32) * key_ref[...]).astype(BF)
     mixed_ref[0] = dot(first_ref[0], scaled).astype(BF)
@@ -56,8 +65,8 @@
 
 def forward_kernel(mixed_ref, second_ref, x_ref, gate_ref, up1, up2, down1, down2, out_ref):
     width = up2.shape[1]
-    x = x_ref[0].astype(F32)
-    _, _, _, hidden = gate_part(mixed_ref[0], second_ref[0], x, gate_ref[...])
+    x = column(x_ref).astype(F32)
+    _, _, _, hidden = gate_part(column(mixed_ref), second_ref[0], x, gate_ref[...])
     permuted = dot(hidden, up1[...]).astype(BF)
     folded = []
     for j in range(up2.shape[0]):
@@ -96,7 +105,7 @@
 ):
     x = x_ref[0].astype(F32)
     grad_ref[0], back_ref[0], direct_ref[0] = backward_body(
-        cot_ref[0], mixed_ref[0], second_ref[0], x, gate_ref[...], up1, up2, down1, down2
+        column(cot_ref), mixed_ref[0], second_ref[0], x, gate_ref[...], up1, up2, down1, down2
     )
 
 
@@ -104,10 +113,10 @@
     direct_ref, scaled_ref, key_ref, mixed_ref, second_ref, x_ref, gate_ref,
     up1, up2, down1, down2, grad_ref, back_ref,
 ):
-    x = x_ref[0].astype(F32)
+    x = column(x_ref).astype(F32)
     cot = (direct_ref[0] + scaled_ref[0].astype(F32) * key_ref[...]).astype(BF)
     grad_ref[0], back_ref[0], _ = backward_body(
-        cot, mixed_ref[0], second_ref[0], x, gate_ref[...], up1, up2, down1, down2
+        cot, column(mixed_ref), second_ref[0], x, gate_ref[...], up1, up2, down1, down2
     )
 
 
@@ -117,6 +126,17 @@
 
 def whole(shape):
     return pl.BlockSpec(tuple(shape), lambda n: (0,) * len(shape))
+
+
+def spec(shape, how):
+    if how is True and len(shape) == 5:
+        return pl.BlockSpec((shape[0], shape[1], 1) + tuple(shape[3:]), lambda n: (0, 0, n, 0, 0))
+    if how is True:
+        return blocked(shape)
+    if how is False:
+        return whole(shape)
+    layer = how[0]
+    return pl.BlockSpec((None,) + tuple(shape[1:]), lambda n: (layer,) + (0,) * (len(shape) - 1))
 
 
 def run(kernel, steps, operands, outs, flops):
@@ -125,7 +145,7 @@
     result = pl.pallas_call(
         kernel,
         grid=(steps,),
-        in_specs=[(blocked if cut else whole)(a.shape) for a, cut in operands],
+        in_specs=[spec(a.shape, how) for a, how in operands],
         out_specs=[blocked(s) for s, _ in outs],
         out_shape=[jax.ShapeDtypeStruct(s, d) for s, d in outs],
         cost_estimate=pl.CostEstimate(flops=flops, bytes_accessed=moved, transcendentals=0),
@@ -145,16 +165,44 @@
     return jnp.swapaxes(got, 0, 1).reshape(full // count, count * own, channels)
 
 
-def turn_split(rows):
-    own, full, channels = rows.shape
+def order_columns(rows):
+    return jnp.swapaxes(rows, 0, 1)
+
+
+def turn_split(sent):
+    full, own, channels = sent.shape
     count = lax.axis_size(ALL)
     parts = lax.axis_size("mp")
-    sent = jnp.swapaxes(rows, 0, 1)
     got = lax.all_to_all(sent, ALL, split_axis=0, concat_axis=0, tiled=True)
     got = got.reshape(count // parts, parts, full // count, own, channels)
+    if own % 16 == 0:
+        return got
     return jnp.transpose(got, (2, 0, 3, 1, 4)).reshape(
         full // count, count // parts * own, parts * channels
     )
+
+
+def swap(pieces, axis):
+    count = lax.axis_size(axis)
+    me = lax.axis_index(axis)
+
+    def chosen(index):
+        piece = pieces[0]
+        for n in range(1, count):
+            piece = jnp.where(index == n, pieces[n], piece)
+        return piece
+
+    held = [chosen(me)]
+    for shift in range(1, count):
+        route = [(n, (n + shift) % count) for n in range(count)]
+        held.append(lax.ppermute(chosen((me + shift) % count), axis, route))
+    result = []
+    for source in range(count):
+        piece = held[0]
+        for shift in range(1, count):
+            piece = jnp.where((me - source) % count == shift, held[shift], piece)
+        result.append(piece)
+    return result
 
 
 def spread_pair(first, last):
@@ -192,16 +240,15 @@
     gains = gains.reshape(2, segments, 1, model)
     keys, gates = gains[0], gains[1]
 
-    first_all = lax.all_to_all(
-        first_factor.reshape(segments, core_rows, size, size), "segment",
-        split_axis=0, concat_axis=0, tiled=True,
-    )
-    first_low = first_all[0]
-    first_high = lax.dynamic_slice_in_dim(first_all[1], part * own, own, 0)
+    first_cut = first_factor.reshape(segments, core_rows, size, size)
+    first_low, first_high = swap([first_cut[n] for n in range(segments)], "segment")
+    first_high = lax.dynamic_slice_in_dim(first_high, part * own, own, 0)
     second_mine = lax.dynamic_index_in_dim(
         second_factor.reshape(segments, parts, own, size, size), part, 1, keepdims=False
     )
-    second_all = lax.all_to_all(second_mine, "segment", split_axis=0, concat_axis=0, tiled=True)
+    second_low_block, second_high_block = swap(
+        [second_mine[n] for n in range(segments)], "segment"
+    )
 
     core_in = lax.dynamic_slice_in_dim(
         inputs.reshape(held, size, channels), segment * core_rows, core_rows, 0
@@ -230,8 +277,7 @@
 
     def ffn(layer):
         return [
-            (wide_up[layer], False), (ups[layer], False),
-            (downs[layer], False), (wide_down[layer], False),
+            (wide_up, (layer,)), (ups, (layer,)), (downs, (layer,)), (wide_down, (layer,)),
         ]
 
     grid_rows = (own, size, model)
@@ -245,13 +291,16 @@
         [(core_in, True), (key_low, False), (first_low, True)],
         [((core_rows, size, channels), BF)], cube,
     )
+    in_cols = turn_split(order_columns(core_in))
+    mixed_low, in_cols = lax.optimization_barrier((order_columns(mixed_low), in_cols))
     mixed_low = turn_split(mixed_low)
-    in_cols = turn_split(core_in)
+    cot_cols = turn_split(order_columns(core_cot))
     (middle,) = run(
         forward_kernel, own,
-        [(mixed_low, True), (second_all[0], True), (in_cols, True), (gates[0], False)] + ffn(0),
+        [(mixed_low, True), (second_low_block, True), (in_cols, True), (gates[0], False)] + ffn(0),
         [(grid_rows, BF)], cube + feed,
     )
+    middle, cot_cols = lax.optimization_barrier((middle, cot_cols))
     middle_rows = turn(middle)
     (mixed_high,) = run(
         rows_kernel, own,
@@ -259,11 +308,10 @@
         [(grid_rows, BF)], cube,
     )
     mixed_high = turn(mixed_high)
-    cot_cols = turn_split(core_cot)
     second_high, back_high, direct = run(
         upper_kernel, own,
         [
-            (cot_cols, True), (mixed_high, True), (second_all[1], True),
+            (cot_cols, True), (mixed_high, True), (second_high_block, True),
             (middle, True), (gates[1], False),
         ] + ffn(1),
         [(grad_shape, BF), (grid_rows, BF), (grid_rows, F32)], 3 * cube + 2 * feed,
@@ -279,11 +327,12 @@
         lower_kernel, own,
         [
             (direct, True), (scaled_cols, True), (keys[1], False), (mixed_low, True),
-            (second_all[0], True), (in_cols, True), (gates[0], False),
+            (second_low_block, True), (in_cols, True), (gates[0], False),
         ] + ffn(0),
         [(grad_shape, BF), (grid_rows, BF)], 3 * cube + 2 * feed,
     )
-    in_rows = lax.all_to_all(core_in, "mp", split_axis=0, concat_axis=2, tiled=True)
+    in_cut = core_in.reshape(parts, own, size, channels)
+    in_rows = jnp.concatenate(swap([in_cut[n] for n in range(parts)], "mp"), axis=2)
     low_rows = turn(back_low)
     (grad_low,) = run(
         rows_grad_kernel, own,
@@ -291,10 +340,12 @@
         [(grad_shape, BF)], cube,
     )
 
+    def halves(grad):
+        cut = grad.reshape(own, parts, size // parts, size)
+        return jnp.stack(swap([cut[:, n] for n in range(parts)], "mp"))
+
     def hand_out(low, high):
-        both = jnp.stack([low, high]).reshape(segments, own, parts, size // parts, size)
-        both = jnp.swapaxes(both, 1, 2).reshape(segments * parts, own, size // parts, size)
-        got = lax.all_to_all(both, ("segment", "mp"), split_axis=0, concat_axis=0, tiled=True)
+        got = jnp.stack(swap([halves(low), halves(high)], "segment"))
         return got.reshape(1, held, size // parts, size).astype(F32)
 
     return hand_out(grad_low, grad_high), hand_out(second_low, second_high)

time: 652 us -> 574 us (0.88); the launches traced: 641 us -> 573 us
  local copies, waits for them, and re-layouts: 103 us -> 52 us
  waiting for transfers between devices: 275 us -> 253 us
  other arithmetic: 10.8 us -> 30.3 us
  starting transfers between devices: 48.4 us -> 31.7 us
    ppermute x0 -> x9, waiting for transfers between devices: none -> 80.9 us  [swap(): held.append(lax.ppermute(chosen((me + shift) % count), axis, route))]
    all_to_all x3, waiting for transfers between devices: 114 us -> 76.4 us  [turn_split(): got = lax.all_to_all(sent, ALL, split_axis=0, concat_axis=0, tiled=True)]
    all_to_all x5 -> x0, waiting for transfers between devices: 33.4 us -> none  [the longest x2 33.4 us: hand_out(): lax.all_to_all(both, ('segment', 'mp'), split_axis=0, concat_axis=0, tile...]
    all_to_all x3, waiting for transfers between devices: 127 us -> 95.5 us  [turn(): got = lax.all_to_all(sent, ALL, split_axis=0, concat_axis=0, tiled=True)]
    all_to_all x5 -> x0, starting transfers between devices: 22.4 us -> none  [the longest x2 8.07 us: hand_out(): lax.all_to_all(both, ('segment', 'mp'), split_axis=0, concat_axis=0, tile...]
    reshape x5 -> x2, local copies, waits for them, and re-layouts: 23.9 us -> 2.91 us  [the longest x1 2.47 us: on_device(): ups = piece[1].reshape(segments, parts * blocks, width, hidden)]
    select_n x0 -> x13, other arithmetic: none -> 18.7 us  [the longest x9 10.1 us: chosen(): piece = jnp.where(index == n, pieces[n], piece)]
    transpose x6 -> x2, local copies, waits for them, and re-layouts: 17.1 us -> 4.27 us  [order_columns(): return jnp.swapaxes(rows, 0, 1)]
  transfers between devices with their start and end apart: 12 -> 16, of which waited for: 8 -> 11; matrix products, arithmetic and copies ran while one was open for 12% -> 8% of each run, Pallas kernels for 5% -> 5%
where the time goes in v2:
time: 574 us; the launch traced here: 573 us
  waiting for transfers between devices  253 us (44%)
  blocking collectives  116 us (20%)
  Pallas kernels  74 us (13%)
  local copies, waits for them, and re-layouts  52 us (9%)
  starting transfers between devices  31.7 us (6%)
  other arithmetic  30.3 us (5%)
  between operations  14.6 us (3%)
    all_to_all x2, blocking collectives, turn(): got = lax.all_to_all(sent, ALL, split_axis=0, concat_axis=0, tiled=True)  104 us
    all_to_all x3, waiting for transfers between devices, turn(): got = lax.all_to_all(sent, ALL, split_axis=0, concat_axis=0, tiled=True)  95.5 us
    ppermute x9, waiting for transfers between devices, swap(): held.append(lax.ppermute(chosen((me + shift) % count), axis, route))  80.9 us
    all_to_all x3, waiting for transfers between devices, turn_split(): got = lax.all_to_all(sent, ALL, split_axis=0, concat_axis=0, tiled=True)  76.4 us
    pallas_call x7, Pallas kernels, run(): pl.pallas_call(kernel, grid=(steps,), in_specs=[spec(a.shape, how) for a,...  74 us
    transpose x5, local copies, waits for them, and re-layouts, turn(): sent = jnp.swapaxes(rows, 0, 1)  14.9 us
    all_to_all x3, starting transfers between devices, turn_split(): got = lax.all_to_all(sent, ALL, split_axis=0, concat_axis=0, tiled=True)  14.9 us
    all_to_all x3, starting transfers between devices, turn(): got = lax.all_to_all(sent, ALL, split_axis=0, concat_axis=0, tiled=True)  11.7 us
  transfers between devices with their start and end apart: 16, of which 11 were waited for; matrix products, arithmetic and copies ran while one was open for 8% of the time, Pallas kernels for 5%

profile of v2, /device:TPU:0, one launch (start us, length us, event | category | flops | bytes accessed | tf_op | source)
XLA Modules:
  0.0 572.6 jit_solution(12300729670844803229)
XLA Ops:
  11.5 7.4 %all-to-all-start = ((bf16[256,16,256]{2,1,0:T(8,128)(2,1)}), bf16[256,16,256]{2,1,0:T(8,128)(2,1)}, u32[]{:S(2)}, u32[]{:S(2)}) async-start(bf16[256,16,256]{2,1,0:T(8,128)(2,1)} %copy.37), calls=%async_computation | async-start | bytes 4194304 | tf_op jit(solution)/shard_map/all_to_all | solution.py:176
  18.9 3.8 select_bitcast_fusion.1
  22.9 11.6 %all-gather.2 = f32[4,2,256]{2,1,0:T(2,128)S(1)} all-gather(f32[1,2,256]{2,1,0:T(2,128)S(1)} %maximum_bitcast_fusion), channel_id=2, replica_groups=mesh['segment'=2,'seq'=8,'mp'=2] {'segment','mp'}, dimensions={0}, use_global_device_ids=true | all-gather | bytes 10240 | tf_op jit(solution)/shard_map/all_gather | solution.py:238
  39.9 9.1 %shard_map.113 = bf16[16,256,256]{2,1,0:T(8,128)(2,1)S(1)} custom-call(bf16[16,256,256]{2,1,0:T(8,128)(2,1)S(1)} %constant_dynamic-slice_fusion.2.x_ref, f32[1,256]{1,0:T(1,128)S(1)} %constant_dynamic-slice_fusion.1.key_ref, bf16[16,256,256]{2,1,0:T(8,128)(2,1)} %get-tuple-element.24.first_ref), custom_call_target="tpu_custom_call" | custom-call | flops 536870912 | bytes 6292480 | tf_op jit(solution)/shard_map/pallas_call | solution.py:145
  49.0 18.6 %all-to-all-done = bf16[256,16,256]{2,1,0:T(8,128)(2,1)} async-done(((bf16[256,16,256]{2,1,0:T(8,128)(2,1)}), bf16[256,16,256]{2,1,0:T(8,128)(2,1)}, u32[]{:S(2)}, u32[]{:S(2)}) %all-to-all-start) | async-done | bytes 2097184 | tf_op jit(solution)/shard_map/all_to_all | solution.py:176
  67.6 2.5 copy.38
  70.1 3.7 all-to-all-start.1
  79.3 43.3 %all-to-all-done.1 = bf16[256,16,256]{2,1,0:T(8,128)(2,1)S(1)} async-done(((bf16[256,16,256]{2,1,0:T(8,128)(2,1)}), bf16[256,16,256]{2,1,0:T(8,128)(2,1)S(1)}, u32[]{:S(2)}, u32[]{:S(2)}) %all-to-all-start.1) | async-done | bytes 2097184 | tf_op jit(solution)/shard_map/all_to_all | solution.py:176
  123.9 3.8 all-to-all-start.2
  132.1 2.7 bitcast_select_fusion
  146.7 15.1 %shard_map.114.x_ref = bf16[8,256,512]{2,1,0:T(8,128)(2,1)} custom-call(bf16[16,2,8,16,256]{4,3,2,1,0:T(8,128)(2,1)} %bitcast.279, bf16[8,256,256]{2,1,0:T(8,128)(2,1)S(1)} %get-tuple-element.29.second_ref, bf16[16,2,8,16,256]{4,3,2,1,0:T(8,128)(2,1)} %bitcast.8.x_ref, f32[1,512]{1,0:T(1,128)S(1)} %bitcast.263, bf16[2,512,512]{2,1,0:T(8,128)(2,1)S(1)} %bitcast.255, ...), custom_call_target="tpu_custom_call" | custom-call | flops 4831838208 | bytes 11536384 | tf_op jit(solution)/shard_map/pallas_call | solution.py:145
  161.8 14.6 %all-to-all-done.2 = bf16[256,16,256]{2,1,0:T(8,128)(2,1)} async-done(((bf16[256,16,256]{2,1,0:T(8,128)(2,1)}), bf16[256,16,256]{2,1,0:T(8,128)(2,1)}, u32[]{:S(2)}, u32[]{:S(2)}) %all-to-all-start.2) | async-done | bytes 2097184 | tf_op jit(solution)/shard_map/all_to_all | solution.py:176
  176.4 4.1 copy.44
  180.4 4.0 all-to-all-start.3
  186.1 46.8 %all-to-all-done.3 = bf16[256,8,512]{2,1,0:T(8,128)(2,1)} async-done(((bf16[256,8,512]{2,1,0:T(8,128)(2,1)}), bf16[256,8,512]{2,1,0:T(8,128)(2,1)}, u32[]{:S(2)}, u32[]{:S(2)}) %all-to-all-start.3) | async-done | bytes 2097184 | tf_op jit(solution)/shard_map/all_to_all | solution.py:163
  239.2 3.8 all-to-all-start.4
  243.0 48.7 %all-to-all-done.4 = bf16[256,8,512]{2,1,0:T(8,128)(2,1)} async-done(((bf16[256,8,512]{2,1,0:T(8,128)(2,1)}), bf16[256,8,512]{2,1,0:T(8,128)(2,1)}, u32[]{:S(2)}, u32[]{:S(2)}) %all-to-all-start.4) | async-done | bytes 2097184 | tf_op jit(solution)/shard_map/all_to_all | solution.py:163
  291.7 3.3 copy.94
  295.0 20.1 %shard_map.116 = (bf16[8,256,256]{2,1,0:T(8,128)(2,1)S(1)}, bf16[8,256,512]{2,1,0:T(8,128)(2,1)}, f32[8,256,512]{2,1,0:T(8,128)}) custom-call(bf16[16,2,8,16,256]{4,3,2,1,0:T(8,128)(2,1)} %bitcast.25.cot_ref, bf16[8,256,512]{2,1,0:T(8,128)(2,1)} %bitcast.284, bf16[8,256,256]{2,1,0:T(8,128)(2,1)S(1)} %copy-done.10, bf16[8,256,512]{2,1,0:T(8,128)(2,1)} %shard_map.114.x_ref, ...), custom_call_target="tpu_custom_call" | custom-call | flops 10200547328 | bytes 18876416 | tf_op jit(solution)/shard_map/pallas_call | solution.py:145
  315.1 3.1 copy.48
  318.2 52.2 %all_to_all.40 = bf16[256,8,512]{2,1,0:T(8,128)(2,1)S(1)} all-to-all(bf16[256,8,512]{2,1,0:T(8,128)(2,1)S(1)} %copy.48), channel_id=1, replica_groups=mesh['segment'=2,'seq'=8,'mp'=2] {'seq','segment','mp'}, dimensions={0} | all-to-all | bytes 4194304 | tf_op jit(solution)/shard_map/all_to_all | solution.py:163
  371.9 5.9 %shard_map.117 = (bf16[8,256,256]{2,1,0:T(8,128)(2,1)S(1)}, bf16[8,256,512]{2,1,0:T(8,128)(2,1)S(1)}) custom-call(bf16[8,256,512]{2,1,0:T(8,128)(2,1)} %bitcast.270, bf16[8,256,512]{2,1,0:T(8,128)(2,1)} %bitcast.242, f32[1,512]{1,0:T(1,128)S(1)} %bitcast.259, bf16[8,256,256]{2,1,0:T(8,128)(2,1)S(1)} %dynamic-slice_select_fusion.first_ref), custom_call_target="tpu_custom_call" | custom-call | flops 1073741824 | bytes 8390656 | tf_op jit(solution)/shard_map/pallas_call | solution.py:145
  379.0 52.2 %all_to_all.41 = bf16[256,8,512]{2,1,0:T(8,128)(2,1)S(1)} all-to-all(bf16[256,8,512]{2,1,0:T(8,128)(2,1)S(1)} %copy.52), channel_id=1, replica_groups=mesh['segment'=2,'seq'=8,'mp'=2] {'seq','segment','mp'}, dimensions={0} | all-to-all | bytes 4194304 | tf_op jit(solution)/shard_map/all_to_all | solution.py:163
  432.7 19.6 %shard_map.118 = (bf16[8,256,256]{2,1,0:T(8,128)(2,1)S(1)}, bf16[8,256,512]{2,1,0:T(8,128)(2,1)}) custom-call(f32[8,256,512]{2,1,0:T(8,128)} %get-tuple-element.19.direct_ref, bf16[8,256,512]{2,1,0:T(8,128)(2,1)} %bitcast.282, f32[1,512]{1,0:T(1,128)S(1)} %bitcast.260, bf16[16,2,8,16,256]{4,3,2,1,0:T(8,128)(2,1)} %bitcast.280, ...), custom_call_target="tpu_custom_call" | custom-call | flops 10200547328 | bytes 18878464 | tf_op jit(solution)/shard_map/pallas_call | solution.py:145
  453.3 4.1 copy.54
  457.4 4.0 all-to-all-start.7
  466.0 43.3 %collective-permute-done.3 = bf16[8,256,256]{2,1,0:T(8,128)(2,1)S(1)} collective-permute-done((bf16[8,256,256]{2,1,0:T(8,128)(2,1)S(1)}, bf16[8,256,256]{2,1,0:T(8,128)(2,1)S(1)}, u32[]{:S(2)}, u32[]{:S(2)}) %collective-permute-start.3) | collective-permute-done | bytes 1048608 | tf_op jit(solution)/shard_map/ppermute | solution.py:198
  511.3 8.9 %collective-permute-done.6 = bf16[8,128,256]{2,1,0:T(8,128)(2,1)} collective-permute-done((bf16[8,128,256]{2,1,0:T(8,128)(2,1)}, bf16[8,128,256]{2,1,0:T(8,128)(2,1)}, u32[]{:S(2)}, u32[]{:S(2)}) %collective-permute-start.6) | collective-permute-done | bytes 524320 | tf_op jit(solution)/shard_map/ppermute | solution.py:198
  530.6 7.8 %collective-permute-done.7 = bf16[8,128,256]{2,1,0:T(8,128)(2,1)} collective-permute-done((bf16[8,128,256]{2,1,0:T(8,128)(2,1)}, bf16[8,128,256]{2,1,0:T(8,128)(2,1)}, u32[]{:S(2)}, u32[]{:S(2)}) %collective-permute-start.7) | collective-permute-done | bytes 524320 | tf_op jit(solution)/shard_map/ppermute | solution.py:198
  539.8 9.8 %collective-permute-done.2 = bf16[8,128,256]{2,1,0:T(8,128)(2,1)} collective-permute-done((bf16[8,128,256]{2,1,0:T(8,128)(2,1)}, bf16[8,128,256]{2,1,0:T(8,128)(2,1)}, u32[]{:S(2)}, u32[]{:S(2)}) %collective-permute-start.2) | collective-permute-done | bytes 524320 | tf_op jit(solution)/shard_map/ppermute | solution.py:198
  550.7 8.6 %collective-permute-done.4 = bf16[8,128,256]{2,1,0:T(8,128)(2,1)S(1)} collective-permute-done((bf16[8,128,256]{2,1,0:T(8,128)(2,1)S(1)}, bf16[8,128,256]{2,1,0:T(8,128)(2,1)S(1)}, u32[]{:S(2)}, u32[]{:S(2)}) %collective-permute-start.4) | collective-permute-done | bytes 524320 | tf_op jit(solution)/shard_map/ppermute | solution.py:198
  560.2 2.5 convert.3
  (133 shorter events, 69.2 us)
Async XLA Ops:
  11.5 56.1 %all-to-all-start = ((bf16[256,16,256]{2,1,0:T(8,128)(2,1)}), bf16[256,16,256]{2,1,0:T(8,128)(2,1)}, u32[]{:S(2)}, u32[]{:S(2)}) async-start(bf16[256,16,256]{2,1,0:T(8,128)(2,1)} %copy.37), calls=%async_computation | async-start | bytes 4194304 | tf_op jit(solution)/shard_map/all_to_all | solution.py:176
  18.9 4.0 copy-start.28
  18.9 4.0 copy-start.29
  22.7 13.8 %collective-permute-start = (bf16[16,256,256]{2,1,0:T(8,128)(2,1)}, bf16[16,256,256]{2,1,0:T(8,128)(2,1)S(1)}, u32[]{:S(2)}, u32[]{:S(2)}) collective-permute-start(bf16[16,256,256]{2,1,0:T(8,128)(2,1)} %select_bitcast_fusion.1), channel_id=1, source_target_pairs={{0,16},{16,0},{1,17},{17,1},{2,18},{18,2},{3,19},{19,3},{4,20},{20... | collective-permute-start | bytes 6291464 | tf_op jit(solution)/shard_map/ppermute | solution.py:198
  70.1 3.7 copy-start.25
  70.1 3.9 copy-start.24
  70.1 3.9 copy-start.26
  70.1 3.9 copy-start.27
  70.1 52.4 %all-to-all-start.1 = ((bf16[256,16,256]{2,1,0:T(8,128)(2,1)}), bf16[256,16,256]{2,1,0:T(8,128)(2,1)S(1)}, u32[]{:S(2)}, u32[]{:S(2)}) async-start(bf16[256,16,256]{2,1,0:T(8,128)(2,1)} %copy.38), calls=%async_computation.1 | async-start | bytes 4194304 | tf_op jit(solution)/shard_map/all_to_all | solution.py:176
  73.8 61.0 %all-gather.5.cloned.1.call-start = ((), (), s32[]{:S(2)}) async-start(), calls=%async_computation.8 | async-start | bytes 3276800 | tf_op jit(solution)/shard_map/all_gather | solution.py:269
  123.9 52.5 %all-to-all-start.2 = ((bf16[256,16,256]{2,1,0:T(8,128)(2,1)}), bf16[256,16,256]{2,1,0:T(8,128)(2,1)}, u32[]{:S(2)}, u32[]{:S(2)}) async-start(bf16[256,16,256]{2,1,0:T(8,128)(2,1)} %bitcast.234), calls=%async_computation.2 | async-start | bytes 4194304 | tf_op jit(solution)/shard_map/all_to_all | solution.py:176
  129.3 2.7 collective-permute-start.1
  134.8 9.5 %copy-start.8 = (bf16[8,256,256]{2,1,0:T(8,128)(2,1)}, bf16[8,256,256]{2,1,0:T(8,128)(2,1)S(1)}, u32[]{:S(2)}) copy-start(bf16[8,256,256]{2,1,0:T(8,128)(2,1)S(1)} %get-tuple-element.29.second_ref) | copy-start | bytes 3145732
  138.1 6.2 %copy-start.11 = (bf16[2,512,512]{2,1,0:T(8,128)(2,1)}, bf16[2,512,512]{2,1,0:T(8,128)(2,1)S(1)}, u32[]{:S(2)}) copy-start(bf16[2,512,512]{2,1,0:T(8,128)(2,1)S(1)} %reshape.168.down2) | copy-start | bytes 3145732
  140.2 4.1 copy-start.12
  180.4 52.5 %all-to-all-start.3 = ((bf16[256,8,512]{2,1,0:T(8,128)(2,1)}), bf16[256,8,512]{2,1,0:T(8,128)(2,1)}, u32[]{:S(2)}, u32[]{:S(2)}) async-start(bf16[256,8,512]{2,1,0:T(8,128)(2,1)} %copy.44), calls=%async_computation.3 | async-start | bytes 4194304 | tf_op jit(solution)/shard_map/all_to_all | solution.py:163
  239.2 52.5 %all-to-all-start.4 = ((bf16[256,8,512]{2,1,0:T(8,128)(2,1)}), bf16[256,8,512]{2,1,0:T(8,128)(2,1)}, u32[]{:S(2)}, u32[]{:S(2)}) async-start(bf16[256,8,512]{2,1,0:T(8,128)(2,1)} %copy.46), calls=%async_computation.4 | async-start | bytes 4194304 | tf_op jit(solution)/shard_map/all_to_all | solution.py:163
  315.1 149.5 %copy-start.6 = (bf16[8,256,256]{2,1,0:T(8,128)(2,1)}, bf16[8,256,256]{2,1,0:T(8,128)(2,1)S(1)}, u32[]{:S(2)}) copy-start(bf16[8,256,256]{2,1,0:T(8,128)(2,1)S(1)} %get-tuple-element.22) | copy-start | bytes 3145732
  457.4 68.7 %all-to-all-start.7 = ((bf16[256,8,512]{2,1,0:T(8,128)(2,1)}), bf16[256,8,512]{2,1,0:T(8,128)(2,1)}, u32[]{:S(2)}, u32[]{:S(2)}) async-start(bf16[256,8,512]{2,1,0:T(8,128)(2,1)} %copy.54), calls=%async_computation.7 | async-start | bytes 4194304 | tf_op jit(solution)/shard_map/all_to_all | solution.py:163
  463.1 46.3 %collective-permute-start.3 = (bf16[8,256,256]{2,1,0:T(8,128)(2,1)S(1)}, bf16[8,256,256]{2,1,0:T(8,128)(2,1)S(1)}, u32[]{:S(2)}, u32[]{:S(2)}) collective-permute-start(bf16[8,256,256]{2,1,0:T(8,128)(2,1)S(1)} %broadcast_select_fusion.5), channel_id=1, source_target_pairs={{0,1},{1,0},{2,3},{3,2},{4,5},{5,4},{6,7},{7,6},{8,9},{9,8},{10,11... | collective-permute-start | bytes 3145736 | tf_op jit(solution)/shard_map/ppermute | solution.py:198
  465.5 54.7 %collective-permute-start.6 = (bf16[8,128,256]{2,1,0:T(8,128)(2,1)}, bf16[8,128,256]{2,1,0:T(8,128)(2,1)}, u32[]{:S(2)}, u32[]{:S(2)}) collective-permute-start(bf16[8,128,256]{2,1,0:T(8,128)(2,1)} %select_bitcast_fusion.8), channel_id=1, source_target_pairs={{0,1},{1,0},{2,3},{3,2},{4,5},{5,4},{6,7},{7,6},{8,9},{9,8},{10,11... | collective-permute-start | bytes 1572872 | tf_op jit(solution)/shard_map/ppermute | solution.py:198
  511.1 9.1 %copy-start.7 = (bf16[8,256,256]{2,1,0:T(8,128)(2,1)S(1)}, bf16[8,256,256]{2,1,0:T(8,128)(2,1)}, u32[]{:S(2)}) copy-start(bf16[8,256,256]{2,1,0:T(8,128)(2,1)} %copy-done.6) | copy-start | bytes 3145732
  511.2 11.1 %copy-start.4 = (bf16[8,256,256]{2,1,0:T(8,128)(2,1)S(1)}, bf16[8,256,256]{2,1,0:T(8,128)(2,1)}, u32[]{:S(2)}) copy-start(bf16[8,256,256]{2,1,0:T(8,128)(2,1)} %copy-done.3) | copy-start | bytes 3145732
  511.3 12.3 %copy-start.2 = (bf16[8,256,256]{2,1,0:T(8,128)(2,1)S(1)}, bf16[8,256,256]{2,1,0:T(8,128)(2,1)}, u32[]{:S(2)}) copy-start(bf16[8,256,256]{2,1,0:T(8,128)(2,1)} %copy-done.1) | copy-start | bytes 3145732
  523.2 15.2 %collective-permute-start.7 = (bf16[8,128,256]{2,1,0:T(8,128)(2,1)}, bf16[8,128,256]{2,1,0:T(8,128)(2,1)}, u32[]{:S(2)}, u32[]{:S(2)}) collective-permute-start(bf16[8,128,256]{2,1,0:T(8,128)(2,1)} %select_bitcast_fusion.7), channel_id=1, source_target_pairs={{0,1},{1,0},{2,3},{3,2},{4,5},{5,4},{6,7},{7,6},{8,9},{9,8},{10,11... | collective-permute-start | bytes 1572872 | tf_op jit(solution)/shard_map/ppermute | solution.py:198
  524.4 25.2 %collective-permute-start.2 = (bf16[8,128,256]{2,1,0:T(8,128)(2,1)}, bf16[8,128,256]{2,1,0:T(8,128)(2,1)}, u32[]{:S(2)}, u32[]{:S(2)}) collective-permute-start(bf16[8,128,256]{2,1,0:T(8,128)(2,1)} %select_bitcast_fusion.11), channel_id=1, source_target_pairs={{0,1},{1,0},{2,3},{3,2},{4,5},{5,4},{6,7},{7,6},{8,9},{9,8},{10,11... | collective-permute-start | bytes 1572872 | tf_op jit(solution)/shard_map/ppermute | solution.py:198
  530.0 8.3 %copy-start.5 = (bf16[8,256,256]{2,1,0:T(8,128)(2,1)S(1)}, bf16[8,256,256]{2,1,0:T(8,128)(2,1)}, u32[]{:S(2)}) copy-start(bf16[8,256,256]{2,1,0:T(8,128)(2,1)} %copy-done.3) | copy-start | bytes 3145732
  530.1 9.4 %copy-start.19 = (bf16[1,8,128,256]{3,2,1,0:T(8,128)(2,1)S(1)}, bf16[1,8,128,256]{3,2,1,0:T(8,128)(2,1)}, u32[]{:S(2)}) copy-start(bf16[1,8,128,256]{3,2,1,0:T(8,128)(2,1)} %get-tuple-element.38) | copy-start | bytes 1572868
  530.1 9.4 %copy-start.20 = (bf16[1,8,128,256]{3,2,1,0:T(8,128)(2,1)S(1)}, bf16[1,8,128,256]{3,2,1,0:T(8,128)(2,1)}, u32[]{:S(2)}) copy-start(bf16[1,8,128,256]{3,2,1,0:T(8,128)(2,1)} %get-tuple-element.39) | copy-start | bytes 1572868
  530.1 29.2 %collective-permute-start.4 = (bf16[8,128,256]{2,1,0:T(8,128)(2,1)S(1)}, bf16[8,128,256]{2,1,0:T(8,128)(2,1)S(1)}, u32[]{:S(2)}, u32[]{:S(2)}) collective-permute-start(bf16[8,128,256]{2,1,0:T(8,128)(2,1)S(1)} %fusion.4), channel_id=1, source_target_pairs={{0,1},{1,0},{2,3},{3,2},{4,5},{5,4},{6,7},{7,6},{8,9},{9,8},{10,11... | collective-permute-start | bytes 1572872 | tf_op jit(solution)/shard_map/ppermute | solution.py:198
  539.7 20.0 %collective-permute-start.8 = (bf16[2,8,128,256]{3,2,1,0:T(8,128)(2,1)S(1)}, bf16[2,8,128,256]{3,2,1,0:T(8,128)(2,1)S(1)}, u32[]{:S(2)}, u32[]{:S(2)}) collective-permute-start(bf16[2,8,128,256]{3,2,1,0:T(8,128)(2,1)S(1)} %broadcast_select_fusion.8), channel_id=1, source_target_pairs={{0,16},{16,0},{1,17},{17,1},{2,18},{18,2},{3,19},{19,3},{4,20},{20... | collective-permute-start | bytes 3145736 | tf_op jit(solution)/shard_map/ppermute | solution.py:198
  559.6 3.1 collective-permute-start.5
  (14 other events, 30.1 us)
Sparse Core Ops, SparseCore 0:
  76.2 35.6 all-gather.4

commit v3 on v2

--- a/solution.py
+++ b/solution.py
@@ -63,7 +63,7 @@
     return turned, gate_pre, sig, hidden
 
 
-def forward_kernel(mixed_ref, second_ref, x_ref, gate_ref, up1, up2, down1, down2, out_ref):
+def forward_kernel(mixed_ref, second_ref, x_ref, gate_ref, up1, up2, down1, down2, out_ref, sent):
     width = up2.shape[1]
     x = column(x_ref).astype(F32)
     _, _, _, hidden = gate_part(column(mixed_ref), second_ref[0], x, gate_ref[...])
@@ -74,7 +74,9 @@
         active = (pre * logistic(pre)).astype(BF)
         folded.append(dot(active, down1[j]).astype(BF))
     folded = jnp.concatenate(folded, axis=1)
-    out_ref[0] = (hidden.astype(F32) + dot(folded, down2[...])).astype(BF)
+    result = (hidden.astype(F32) + dot(folded, down2[...])).astype(BF)
+    out_ref[0] = result
+    sent[0] = result
 
 
 def backward_body(cot, mixed, second, x, gate, up1, up2, down1, down2):
@@ -101,7 +103,7 @@
 
 def upper_kernel(
     cot_ref, mixed_ref, second_ref, x_ref, gate_ref, up1, up2, down1, down2,
-    grad_ref, back_ref, direct_ref,
+    grad_ref, direct_ref, back_ref,
 ):
     x = x_ref[0].astype(F32)
     grad_ref[0], back_ref[0], direct_ref[0] = backward_body(
@@ -156,13 +158,102 @@
     return result
 
 
-def turn(rows):
-    own, full, channels = rows.shape
-    count = lax.axis_size(ALL)
-    sent = jnp.swapaxes(rows, 0, 1)
-    got = lax.all_to_all(sent, ALL, split_axis=0, concat_axis=0, tiled=True)
-    got = got.reshape(count, full // count, own, channels)
-    return jnp.swapaxes(got, 0, 1).reshape(full // count, count * own, channels)
+class Outgoing:
+    def __init__(self, ref, step):
+        self.ref, self.step = ref, step
+
+    def __setitem__(self, _, rows):
+        count, _, own, channels = self.ref.shape
+        self.ref[:, self.step] = rows.reshape(count, own, channels)
+
+
+def run_and_turn(kernel, steps, operands, outs, flops, channels, collective_id):
+    parts, segments, seqs = lax.axis_size("mp"), lax.axis_size("segment"), lax.axis_size("seq")
+    count = parts * segments * seqs
+    own = steps
+    group = max(1, own // 4)
+    n_in, n_out = len(operands), len(outs)
+
+    def body(*refs):
+        got = refs[n_in + n_out]
+        slots, send_sem, recv_sem, own_sem = refs[n_in + n_out + 1 :]
+        step = pl.program_id(0)
+        me = (lax.axis_index("seq") * segments + lax.axis_index("segment")) * parts + lax.axis_index("mp")
+
+        def place(k):
+            device = lax.rem(me + k, count)
+            return device, {
+                "segment": lax.rem(device // parts, segments),
+                "seq": device // (parts * segments),
+                "mp": lax.rem(device, parts),
+            }
+
+        barrier = pltpu.get_barrier_semaphore()
+
+        @pl.when(step == 0)
+        def _():
+            @pl.loop(1, count)
+            def _(k):
+                pl.semaphore_signal(
+                    barrier, inc=1, device_id=place(k)[1], device_id_type=pl.DeviceIdType.MESH
+                )
+
+        kernel(*refs[: n_in + n_out], Outgoing(slots, step))
+
+        @pl.when(step == group - 1)
+        def _():
+            pl.semaphore_wait(barrier, count - 1)
+
+        @pl.when(lax.rem(step, group) == group - 1)
+        def _():
+            base = step - (group - 1)
+            target = got.at[pl.ds(me * own + base, group)]
+
+            @pl.loop(1, count)
+            def _(k):
+                device, where = place(k)
+                pltpu.make_async_remote_copy(
+                    src_ref=slots.at[device, pl.ds(base, group)],
+                    dst_ref=target,
+                    send_sem=send_sem,
+                    recv_sem=recv_sem,
+                    device_id=where,
+                    device_id_type=pl.DeviceIdType.MESH,
+                ).start()
+
+        @pl.when(step == own - 1)
+        def _():
+            mine = pltpu.make_async_copy(slots.at[me], got.at[pl.ds(me * own, own)], own_sem)
+            mine.start()
+            mine.wait()
+            others = slots.at[pl.ds(0, count - 1)]
+            pltpu.make_async_copy(others, others, send_sem).wait()
+            arrived = got.at[pl.ds(0, (count - 1) * own)]
+            pltpu.make_async_copy(arrived, arrived, recv_sem).wait()
+
+    moved = sum(a.size * a.dtype.itemsize for a, _ in operands)
+    result = pl.pallas_call(
+        body,
+        grid=(steps,),
+        in_specs=[spec(a.shape, how) for a, how in operands],
+        out_specs=[blocked(s) for s, _ in outs] + [pl.BlockSpec(memory_space=pl.ANY)],
+        out_shape=[jax.ShapeDtypeStruct(s, d) for s, d in outs]
+        + [jax.ShapeDtypeStruct((count * own, own, channels), BF)],
+        scratch_shapes=[
+            pltpu.VMEM((count, own, own, channels), BF),
+            pltpu.SemaphoreType.DMA,
+            pltpu.SemaphoreType.DMA,
+            pltpu.SemaphoreType.DMA,
+        ],
+        cost_estimate=pl.CostEstimate(
+            flops=flops, bytes_accessed=moved + 150_000_000, transcendentals=0
+        ),
+        compiler_params=pltpu.CompilerParams(
+            vmem_limit_bytes=VMEM_LIMIT, dimension_semantics=("arbitrary",),
+            collective_id=collective_id, has_side_effects=True,
+        ),
+    )(*[a for a, _ in operands])
+    return list(result[:-1]) + [jnp.swapaxes(result[-1], 0, 1)]
 
 
 def order_columns(rows):
@@ -285,6 +376,10 @@
     cube = 2 * own * size * size * model
     feed = 2 * own * size * model * (2 * model + 2 * hidden)
 
+    def halves(grad):
+        cut = grad.reshape(own, parts, size // parts, size)
+        return jnp.stack(swap([cut[:, n] for n in range(parts)], "mp"))
+
     key_low = lax.dynamic_slice_in_dim(keys[0], part * channels, channels, 1)
     (mixed_low,) = run(
         rows_kernel, core_rows,
@@ -295,57 +390,54 @@
     mixed_low, in_cols = lax.optimization_barrier((order_columns(mixed_low), in_cols))
     mixed_low = turn_split(mixed_low)
     cot_cols = turn_split(order_columns(core_cot))
-    (middle,) = run(
+    middle, middle_rows = run_and_turn(
         forward_kernel, own,
         [(mixed_low, True), (second_low_block, True), (in_cols, True), (gates[0], False)] + ffn(0),
-        [(grid_rows, BF)], cube + feed,
-    )
-    middle, cot_cols = lax.optimization_barrier((middle, cot_cols))
-    middle_rows = turn(middle)
-    (mixed_high,) = run(
+        [(grid_rows, BF)], cube + feed, model, 0,
+    )
+    middle_rows, cot_cols = lax.optimization_barrier((middle_rows, cot_cols))
+    (mixed_high,) = run_and_turn(
         rows_kernel, own,
         [(middle_rows, True), (keys[1], False), (first_high, True)],
-        [(grid_rows, BF)], cube,
-    )
-    mixed_high = turn(mixed_high)
-    second_high, back_high, direct = run(
+        [], cube, model, 1,
+    )
+    second_high, direct, back_rows = run_and_turn(
         upper_kernel, own,
         [
             (cot_cols, True), (mixed_high, True), (second_high_block, True),
             (middle, True), (gates[1], False),
         ] + ffn(1),
-        [(grad_shape, BF), (grid_rows, BF), (grid_rows, F32)], 3 * cube + 2 * feed,
-    )
-    back_rows = turn(back_high)
-    grad_high, back_scaled = run(
+        [(grad_shape, BF), (grid_rows, F32)], 3 * cube + 2 * feed, model, 2,
+    )
+    grad_high, scaled_cols = run_and_turn(
         rows_back_kernel, own,
         [(back_rows, True), (middle_rows, True), (keys[1], False), (first_high, True)],
-        [(grad_shape, BF), (grid_rows, BF)], 2 * cube,
-    )
-    scaled_cols = turn(back_scaled)
-    second_low, back_low = run(
+        [(grad_shape, BF)], 2 * cube, model, 3,
+    )
+    in_cut = core_in.reshape(parts, own, size, channels)
+    in_rows = jnp.concatenate(swap([in_cut[n] for n in range(parts)], "mp"), axis=2)
+    second_high = halves(second_high)
+    scaled_cols, in_rows, second_high = lax.optimization_barrier(
+        (scaled_cols, in_rows, second_high)
+    )
+    grad_high = halves(grad_high)
+    second_low, low_rows = run_and_turn(
         lower_kernel, own,
         [
             (direct, True), (scaled_cols, True), (keys[1], False), (mixed_low, True),
             (second_low_block, True), (in_cols, True), (gates[0], False),
         ] + ffn(0),
-        [(grad_shape, BF), (grid_rows, BF)], 3 * cube + 2 * feed,
-    )
-    in_cut = core_in.reshape(parts, own, size, channels)
-    in_rows = jnp.concatenate(swap([in_cut[n] for n in range(parts)], "mp"), axis=2)
-    low_rows = turn(back_low)
+        [(grad_shape, BF)], 3 * cube + 2 * feed, model, 4,
+    )
+    low_rows, grad_high = lax.optimization_barrier((low_rows, grad_high))
     (grad_low,) = run(
         rows_grad_kernel, own,
         [(low_rows, True), (in_rows, True), (keys[0], False)],
         [(grad_shape, BF)], cube,
     )
 
-    def halves(grad):
-        cut = grad.reshape(own, parts, size // parts, size)
-        return jnp.stack(swap([cut[:, n] for n in range(parts)], "mp"))
-
     def hand_out(low, high):
-        got = jnp.stack(swap([halves(low), halves(high)], "segment"))
+        got = jnp.stack(swap([halves(low), high], "segment"))
         return got.reshape(1, held, size // parts, size).astype(F32)
 
     return hand_out(grad_low, grad_high), hand_out(second_low, second_high)

time: 574 us -> 483 us (0.84)
  Pallas kernels: 74 us -> 285 us
  waiting for transfers between devices: 253 us -> 80.8 us
  blocking collectives: 116 us -> 11.6 us
  local copies, waits for them, and re-layouts: 52 us -> 40.7 us
  starting transfers between devices: 31.7 us -> 22.7 us
  other arithmetic: 30.3 us -> 23.1 us
    pallas_call x0 -> x5, Pallas kernels: none -> 274 us  [run_and_turn(): pl.pallas_call(body, grid=(steps,), in_specs=[spec(a.shape, how) for a, h...]
    all_to_all x2 -> x0, blocking collectives: 104 us -> none  [turn(): got = lax.all_to_all(sent, ALL, split_axis=0, concat_axis=0, tiled=True)]
    all_to_all x3 -> x0, waiting for transfers between devices: 95.5 us -> none  [turn(): got = lax.all_to_all(sent, ALL, split_axis=0, concat_axis=0, tiled=True)]
    pallas_call x7 -> x2, Pallas kernels: 74 us -> 11.3 us  [run(): pl.pallas_call(kernel, grid=(steps,), in_specs=[spec(a.shape, how) for a,...]
    ppermute x9, waiting for transfers between devices: 80.9 us -> 19 us  [swap(): held.append(lax.ppermute(chosen((me + shift) % count), axis, route))]
    transpose x5 -> x0, local copies, waits for them, and re-layouts: 14.9 us -> none  [turn(): sent = jnp.swapaxes(rows, 0, 1)]
    all_to_all x3, waiting for transfers between devices: 76.4 us -> 61.8 us  [turn_split(): got = lax.all_to_all(sent, ALL, split_axis=0, concat_axis=0, tiled=True)]
    all_to_all x3 -> x0, starting transfers between devices: 11.7 us -> none  [turn(): got = lax.all_to_all(sent, ALL, split_axis=0, concat_axis=0, tiled=True)]
  transfers between devices with their start and end apart: 16 -> 13, of which waited for: 11 -> 4; matrix products, arithmetic and copies ran while one was open for 8% -> 10% of each run, Pallas kernels for 5% -> 59%
where the time goes in v3:
time: 483 us; the launch traced here: 480 us
  Pallas kernels  285 us (59%)
  waiting for transfers between devices  80.8 us (17%)
  local copies, waits for them, and re-layouts  40.7 us (8%)
  other arithmetic  23.1 us (5%)
  starting transfers between devices  22.7 us (5%)
  between operations  14.7 us (3%)
  blocking collectives  11.6 us (2%)
    pallas_call x5, Pallas kernels, run_and_turn(): pl.pallas_call(body, grid=(steps,), in_specs=[spec(a.shape, how) for a, h...  274 us
    all_to_all x3, waiting for transfers between devices, turn_split(): got = lax.all_to_all(sent, ALL, split_axis=0, concat_axis=0, tiled=True)  61.8 us
    ppermute x9, waiting for transfers between devices, swap(): held.append(lax.ppermute(chosen((me + shift) % count), axis, route))  19 us
    all_to_all x3, starting transfers between devices, turn_split(): got = lax.all_to_all(sent, ALL, split_axis=0, concat_axis=0, tiled=True)  15 us
    unnamed x58, local copies, waits for them, and re-layouts  11.7 us
    all_gather x1, blocking collectives, on_device(): gains = lax.all_gather(gains, ('segment', 'mp'), axis=0, tiled=False)  11.6 us
    pallas_call x2, Pallas kernels, run(): pl.pallas_call(kernel, grid=(steps,), in_specs=[spec(a.shape, how) for a,...  11.3 us
  transfers between devices with their start and end apart: 13, of which 4 were waited for; matrix products, arithmetic and copies ran while one was open for 10% of the time, Pallas kernels for 59%

profile of v3, /device:TPU:0, one launch (start us, length us, event | category | flops | bytes accessed | tf_op | source)
XLA Modules:
  0.0 479.8 jit_solution(10398847377560954059)
XLA Ops:
  8.9 2.6 copy.37
  11.5 7.4 %all-to-all-start = ((bf16[256,16,256]{2,1,0:T(8,128)(2,1)}), bf16[256,16,256]{2,1,0:T(8,128)(2,1)}, u32[]{:S(2)}, u32[]{:S(2)}) async-start(bf16[256,16,256]{2,1,0:T(8,128)(2,1)} %copy.37), calls=%async_computation | async-start | bytes 4194304 | tf_op jit(solution)/shard_map/all_to_all | solution.py:267
  18.9 3.8 select_bitcast_fusion.1
  22.9 11.6 %all-gather.2 = f32[4,2,256]{2,1,0:T(2,128)S(1)} all-gather(f32[1,2,256]{2,1,0:T(2,128)S(1)} %maximum_bitcast_fusion), channel_id=2, replica_groups=mesh['segment'=2,'seq'=8,'mp'=2] {'segment','mp'}, dimensions={0}, use_global_device_ids=true | all-gather | bytes 10240 | tf_op jit(solution)/shard_map/all_gather | solution.py:329
  34.5 1.9 constant_dynamic-slice_fusion.2.x_ref
  37.3 2.5 broadcast_select_fusion
  40.0 9.1 %shard_map.113 = bf16[16,256,256]{2,1,0:T(8,128)(2,1)S(1)} custom-call(bf16[16,256,256]{2,1,0:T(8,128)(2,1)S(1)} %constant_dynamic-slice_fusion.2.x_ref, f32[1,256]{1,0:T(1,128)S(1)} %constant_dynamic-slice_fusion.1.key_ref, bf16[16,256,256]{2,1,0:T(8,128)(2,1)} %get-tuple-element.38.first_ref), custom_call_target="tpu_custom_call" | custom-call | flops 536870912 | bytes 6292480 | tf_op jit(solution)/shard_map/pallas_call | solution.py:147
  49.1 18.5 %all-to-all-done = bf16[256,16,256]{2,1,0:T(8,128)(2,1)} async-done(((bf16[256,16,256]{2,1,0:T(8,128)(2,1)}), bf16[256,16,256]{2,1,0:T(8,128)(2,1)}, u32[]{:S(2)}, u32[]{:S(2)}) %all-to-all-start) | async-done | bytes 2097184 | tf_op jit(solution)/shard_map/all_to_all | solution.py:267
  67.6 2.6 copy.38
  70.2 3.7 all-to-all-start.1
  75.0 1.7 constant_dynamic-slice_fusion
  76.8 2.5 copy.85
  79.3 43.3 %all-to-all-done.1 = bf16[256,16,256]{2,1,0:T(8,128)(2,1)S(1)} async-done(((bf16[256,16,256]{2,1,0:T(8,128)(2,1)}), bf16[256,16,256]{2,1,0:T(8,128)(2,1)S(1)}, u32[]{:S(2)}, u32[]{:S(2)}) %all-to-all-start.1) | async-done | bytes 2097184 | tf_op jit(solution)/shard_map/all_to_all | solution.py:267
  124.0 4.0 all-to-all-start.2
  129.7 2.7 broadcast_select_fusion.5
  134.2 2.8 bitcast_select_fusion
  146.0 2.5 reshape.137.refs_5_.refs_6_.refs_8_
  152.2 67.1 %shard_map.114 = (bf16[8,256,512]{2,1,0:T(8,128)(2,1)}, bf16[256,8,512]{2,1,0:T(8,128)(2,1)}) custom-call(bf16[16,2,8,16,256]{4,3,2,1,0:T(8,128)(2,1)} %bitcast.255, bf16[8,256,256]{2,1,0:T(8,128)(2,1)S(1)} %get-tuple-element.43.refs_1_.refs_4_, bf16[16,2,8,16,256]{4,3,2,1,0:T(8,128)(2,1)} %bitcast.8.refs_2_.refs_5_, f32[1,512]{1,0:T(1,128)S(1)} %bitcast.241, ...), custom_call_target="tpu_custom_call" | custom-call | flops 4831838208 | bytes 159439232 | tf_op jit(solution)/shard_map/pallas_call | solution.py:235
  219.3 2.3 copy.90
  221.6 49.3 %shard_map.115 = bf16[256,8,512]{2,1,0:T(8,128)(2,1)S(1)} custom-call(bf16[8,256,512]{2,1,0:T(8,128)(2,1)S(1)} %bitcast.221, f32[1,512]{1,0:T(1,128)S(1)} %bitcast.236, bf16[8,256,256]{2,1,0:T(8,128)(2,1)S(1)} %dynamic-slice_select_fusion.refs_2_.refs_3_), custom_call_target="tpu_custom_call" | custom-call | flops 536870912 | bytes 153147776 | tf_op jit(solution)/shard_map/pallas_call | solution.py:235
  270.9 2.0 copy.89
  273.8 53.1 %shard_map.116 = (bf16[8,256,256]{2,1,0:T(8,128)(2,1)S(1)}, f32[8,256,512]{2,1,0:T(8,128)}, bf16[256,8,512]{2,1,0:T(8,128)(2,1)}) custom-call(bf16[16,2,8,16,256]{4,3,2,1,0:T(8,128)(2,1)} %bitcast.26.refs_0_, bf16[8,256,512]{2,1,0:T(8,128)(2,1)} %bitcast.258, bf16[8,256,256]{2,1,0:T(8,128)(2,1)S(1)} %copy-done.3, ...), custom_call_target="tpu_custom_call" | custom-call | flops 10200547328 | bytes 161536384 | tf_op jit(solution)/shard_map/pallas_call | solution.py:235
  331.4 2.0 copy.88
  333.4 51.8 %shard_map.117 = (bf16[8,256,256]{2,1,0:T(8,128)(2,1)S(1)}, bf16[256,8,512]{2,1,0:T(8,128)(2,1)S(1)}) custom-call(bf16[8,256,512]{2,1,0:T(8,128)(2,1)} %bitcast.248, bf16[8,256,512]{2,1,0:T(8,128)(2,1)} %bitcast.222, f32[1,512]{1,0:T(1,128)S(1)} %bitcast.237, bf16[8,256,256]{2,1,0:T(8,128)(2,1)S(1)} %dynamic-slice_select_fusion.refs_2_.refs_3_), custom_call_target="tpu_custom_call" | custom-call | flops 1073741824 | bytes 155244928 | tf_op jit(solution)/shard_map/pallas_call | solution.py:235
  385.2 2.0 copy.87
  388.6 52.4 %shard_map.118 = (bf16[8,256,256]{2,1,0:T(8,128)(2,1)S(1)}, bf16[256,8,512]{2,1,0:T(8,128)(2,1)}) custom-call(f32[8,256,512]{2,1,0:T(8,128)} %get-tuple-element.26.refs_0_, bf16[8,256,512]{2,1,0:T(8,128)(2,1)} %bitcast.257, f32[1,512]{1,0:T(1,128)S(1)} %bitcast.238, bf16[16,2,8,16,256]{4,3,2,1,0:T(8,128)(2,1)} %bitcast.256, ...), custom_call_target="tpu_custom_call" | custom-call | flops 10200547328 | bytes 165732736 | tf_op jit(solution)/shard_map/pallas_call | solution.py:235
  441.1 1.8 collective-permute-start.7
  443.8 2.2 shard_map.119
  447.5 8.4 %collective-permute-done.7 = bf16[8,128,256]{2,1,0:T(8,128)(2,1)S(1)} collective-permute-done((bf16[8,128,256]{2,1,0:T(8,128)(2,1)S(1)}, bf16[8,128,256]{2,1,0:T(8,128)(2,1)S(1)}, u32[]{:S(2)}, u32[]{:S(2)}) %collective-permute-start.7) | collective-permute-done | bytes 524320 | tf_op jit(solution)/shard_map/ppermute | solution.py:289
  456.2 10.5 %collective-permute-done.5 = bf16[8,128,256]{2,1,0:T(8,128)(2,1)S(1)} collective-permute-done((bf16[8,128,256]{2,1,0:T(8,128)(2,1)S(1)}, bf16[8,128,256]{2,1,0:T(8,128)(2,1)S(1)}, u32[]{:S(2)}, u32[]{:S(2)}) %collective-permute-start.5) | collective-permute-done | bytes 524320 | tf_op jit(solution)/shard_map/ppermute | solution.py:289
  467.5 2.5 convert.3
  470.4 2.5 convert.2
  (114 shorter events, 32.0 us)
Async XLA Ops:
  11.5 56.1 %all-to-all-start = ((bf16[256,16,256]{2,1,0:T(8,128)(2,1)}), bf16[256,16,256]{2,1,0:T(8,128)(2,1)}, u32[]{:S(2)}, u32[]{:S(2)}) async-start(bf16[256,16,256]{2,1,0:T(8,128)(2,1)} %copy.37), calls=%async_computation | async-start | bytes 4194304 | tf_op jit(solution)/shard_map/all_to_all | solution.py:267
  18.9 4.0 copy-start.24
  18.9 4.0 copy-start.25
  22.7 13.8 %collective-permute-start = (bf16[16,256,256]{2,1,0:T(8,128)(2,1)}, bf16[16,256,256]{2,1,0:T(8,128)(2,1)S(1)}, u32[]{:S(2)}, u32[]{:S(2)}) collective-permute-start(bf16[16,256,256]{2,1,0:T(8,128)(2,1)} %select_bitcast_fusion.1), channel_id=1, source_target_pairs={{0,16},{16,0},{1,17},{17,1},{2,18},{18,2},{3,19},{19,3},{4,20},{20... | collective-permute-start | bytes 6291464 | tf_op jit(solution)/shard_map/ppermute | solution.py:289
  34.5 2.8 copy-start.12
  37.3 2.6 copy-start.13
  70.2 3.7 copy-start.21
  70.2 3.9 copy-start.20
  70.2 3.9 copy-start.22
  70.2 3.9 copy-start.23
  70.2 52.4 %all-to-all-start.1 = ((bf16[256,16,256]{2,1,0:T(8,128)(2,1)}), bf16[256,16,256]{2,1,0:T(8,128)(2,1)S(1)}, u32[]{:S(2)}, u32[]{:S(2)}) async-start(bf16[256,16,256]{2,1,0:T(8,128)(2,1)} %copy.38), calls=%async_computation.1 | async-start | bytes 4194304 | tf_op jit(solution)/shard_map/all_to_all | solution.py:267
  73.9 63.3 %all-gather.5.cloned.1.call-start = ((), (), s32[]{:S(2)}) async-start(), calls=%async_computation.3 | async-start | bytes 3276800 | tf_op jit(solution)/shard_map/all_gather | solution.py:360
  124.0 97.6 %all-to-all-start.2 = ((bf16[256,16,256]{2,1,0:T(8,128)(2,1)}), bf16[256,16,256]{2,1,0:T(8,128)(2,1)}, u32[]{:S(2)}, u32[]{:S(2)}) async-start(bf16[256,16,256]{2,1,0:T(8,128)(2,1)} %bitcast.214), calls=%async_computation.2 | async-start | bytes 4194304 | tf_op jit(solution)/shard_map/all_to_all | solution.py:267
  129.6 4.5 collective-permute-start.1
  132.4 195.9 %collective-permute-start.2 = (bf16[8,256,256]{2,1,0:T(8,128)(2,1)}, bf16[8,256,256]{2,1,0:T(8,128)(2,1)}, u32[]{:S(2)}, u32[]{:S(2)}) collective-permute-start(bf16[8,256,256]{2,1,0:T(8,128)(2,1)} %broadcast_select_fusion.5), channel_id=1, source_target_pairs={{0,1},{1,0},{2,3},{3,2},{4,5},{5,4},{6,7},{7,6},{8,9},{9,8},{10,11... | collective-permute-start | bytes 3145736 | tf_op jit(solution)/shard_map/ppermute | solution.py:289
  134.1 2.9 copy-start.14
  134.1 2.9 copy-start.15
  137.0 11.5 %copy-start.1 = (bf16[8,256,256]{2,1,0:T(8,128)(2,1)}, bf16[8,256,256]{2,1,0:T(8,128)(2,1)S(1)}, u32[]{:S(2)}) copy-start(bf16[8,256,256]{2,1,0:T(8,128)(2,1)S(1)} %get-tuple-element.43.refs_1_.refs_4_) | copy-start | bytes 3145732
  142.0 6.5 %copy-start.4 = (bf16[2,512,512]{2,1,0:T(8,128)(2,1)}, bf16[2,512,512]{2,1,0:T(8,128)(2,1)S(1)}, u32[]{:S(2)}) copy-start(bf16[2,512,512]{2,1,0:T(8,128)(2,1)S(1)} %reshape.138.refs_7_.refs_8_.refs_10_) | copy-start | bytes 3145732
  142.0 2.5 copy-start.16
  221.6 49.3 %copy-start = (bf16[256,8,512]{2,0,1:T(8,128)(2,1)}, bf16[256,8,512]{2,0,1:T(8,128)(2,1)S(1)}, u32[]{:S(2)}) copy-start(bf16[256,8,512]{2,0,1:T(8,128)(2,1)S(1)} %copy.90) | copy-start | bytes 6291460
  270.9 2.1 copy-start.3
  270.9 2.1 copy-start.6
  270.9 2.3 copy-start.8
  270.9 2.9 copy-start.10
  273.8 54.5 %copy-start.11 = (bf16[8192,256]{1,0:T(8,128)(2,1)S(1)}, bf16[8192,256]{1,0:T(8,128)(2,1)}, u32[]{:S(2)}) copy-start(bf16[8192,256]{1,0:T(8,128)(2,1)} %param.10) | copy-start | bytes 12582916
  327.0 61.4 %collective-permute-start.3 = (bf16[8,128,256]{2,1,0:T(8,128)(2,1)S(1)}, bf16[8,128,256]{2,1,0:T(8,128)(2,1)S(1)}, u32[]{:S(2)}, u32[]{:S(2)}) collective-permute-start(bf16[8,128,256]{2,1,0:T(8,128)(2,1)S(1)} %select_bitcast_fusion.11), channel_id=1, source_target_pairs={{0,1},{1,0},{2,3},{3,2},{4,5},{5,4},{6,7},{7,6},{8,9},{9,8},{10,11... | collective-permute-start | bytes 1572872 | tf_op jit(solution)/shard_map/ppermute | solution.py:289
  387.3 55.6 %collective-permute-start.4 = (bf16[8,128,256]{2,1,0:T(8,128)(2,1)S(1)}, bf16[8,128,256]{2,1,0:T(8,128)(2,1)S(1)}, u32[]{:S(2)}, u32[]{:S(2)}) collective-permute-start(bf16[8,128,256]{2,1,0:T(8,128)(2,1)S(1)} %select_bitcast_fusion.10), channel_id=1, source_target_pairs={{0,1},{1,0},{2,3},{3,2},{4,5},{5,4},{6,7},{7,6},{8,9},{9,8},{10,11... | collective-permute-start | bytes 1572872 | tf_op jit(solution)/shard_map/ppermute | solution.py:289
  441.1 14.8 %collective-permute-start.7 = (bf16[8,128,256]{2,1,0:T(8,128)(2,1)S(1)}, bf16[8,128,256]{2,1,0:T(8,128)(2,1)S(1)}, u32[]{:S(2)}, u32[]{:S(2)}) collective-permute-start(bf16[8,128,256]{2,1,0:T(8,128)(2,1)S(1)} %select_bitcast_fusion.7), channel_id=1, source_target_pairs={{0,1},{1,0},{2,3},{3,2},{4,5},{5,4},{6,7},{7,6},{8,9},{9,8},{10,11... | collective-permute-start | bytes 1572872 | tf_op jit(solution)/shard_map/ppermute | solution.py:289
  446.1 20.7 %collective-permute-start.5 = (bf16[8,128,256]{2,1,0:T(8,128)(2,1)S(1)}, bf16[8,128,256]{2,1,0:T(8,128)(2,1)S(1)}, u32[]{:S(2)}, u32[]{:S(2)}) collective-permute-start(bf16[8,128,256]{2,1,0:T(8,128)(2,1)S(1)} %fusion.4), channel_id=1, source_target_pairs={{0,1},{1,0},{2,3},{3,2},{4,5},{5,4},{6,7},{7,6},{8,9},{9,8},{10,11... | collective-permute-start | bytes 1572872 | tf_op jit(solution)/shard_map/ppermute | solution.py:289
  456.1 10.9 %collective-permute-start.8 = (bf16[2,8,128,256]{3,2,1,0:T(8,128)(2,1)S(1)}, bf16[2,8,128,256]{3,2,1,0:T(8,128)(2,1)S(1)}, u32[]{:S(2)}, u32[]{:S(2)}) collective-permute-start(bf16[2,8,128,256]{3,2,1,0:T(8,128)(2,1)S(1)} %broadcast_select_fusion.8), channel_id=1, source_target_pairs={{0,16},{16,0},{1,17},{17,1},{2,18},{18,2},{3,19},{19,3},{4,20},{20... | collective-permute-start | bytes 3145736 | tf_op jit(solution)/shard_map/ppermute | solution.py:289
  467.0 3.0 collective-permute-start.6
  (7 other events, 9.9 us)
Sparse Core Ops, SparseCore 0:
  76.2 35.6 all-gather.4

commit v4 on v3

--- a/solution.py
+++ b/solution.py
@@ -63,7 +63,7 @@
     return turned, gate_pre, sig, hidden
 
 
-def forward_kernel(mixed_ref, second_ref, x_ref, gate_ref, up1, up2, down1, down2, out_ref, sent):
+def forward_kernel(second_ref, mixed_ref, x_ref, gate_ref, up1, up2, down1, down2, out_ref, sent):
     width = up2.shape[1]
     x = column(x_ref).astype(F32)
     _, _, _, hidden = gate_part(column(mixed_ref), second_ref[0], x, gate_ref[...])
@@ -102,7 +102,7 @@
 
 
 def upper_kernel(
-    cot_ref, mixed_ref, second_ref, x_ref, gate_ref, up1, up2, down1, down2,
+    second_ref, cot_ref, mixed_ref, x_ref, gate_ref, up1, up2, down1, down2,
     grad_ref, direct_ref, back_ref,
 ):
     x = x_ref[0].astype(F32)
@@ -112,7 +112,7 @@
 
 
 def lower_kernel(
-    direct_ref, scaled_ref, key_ref, mixed_ref, second_ref, x_ref, gate_ref,
+    direct_ref, scaled_ref, key_ref, second_ref, mixed_ref, x_ref, gate_ref,
     up1, up2, down1, down2, grad_ref, back_ref,
 ):
     x = column(x_ref).astype(F32)
@@ -167,24 +167,50 @@
         self.ref[:, self.step] = rows.reshape(count, own, channels)
 
 
-def run_and_turn(kernel, steps, operands, outs, flops, channels, collective_id):
+class Handed:
+    def __init__(self, ref, step):
+        self.ref, self.step = ref, step
+
+    def __setitem__(self, _, grad):
+        self.ref[self.step] = grad
+
+
+def run_and_send(kernel, steps, operands, outs, flops, collective_id, channels=0, layer=None, group=1):
     parts, segments, seqs = lax.axis_size("mp"), lax.axis_size("segment"), lax.axis_size("seq")
     count = parts * segments * seqs
+    near = parts * segments
     own = steps
-    group = max(1, own // 4)
+    group = min(group, own)
+    size = operands[0][0].shape[1]
+    half = size // parts
     n_in, n_out = len(operands), len(outs)
+    turns, hands = channels > 0, layer is not None
 
     def body(*refs):
-        got = refs[n_in + n_out]
-        slots, send_sem, recv_sem, own_sem = refs[n_in + n_out + 1 :]
+        refs = list(refs)
+        ins, refs = refs[:n_in], refs[n_in:]
+        local, refs = refs[:n_out], refs[n_out:]
+        got = refs.pop(0) if turns else None
+        grads = refs.pop(0) if hands else None
+        if turns:
+            slots, send_sem, recv_sem, own_sem = refs[:4]
+            refs = refs[4:]
+        if hands:
+            held, grad_send, grad_recv, grad_own = refs
         step = pl.program_id(0)
-        me = (lax.axis_index("seq") * segments + lax.axis_index("segment")) * parts + lax.axis_index("mp")
+        segment, part = lax.axis_index("segment"), lax.axis_index("mp")
+        me_near = segment * parts + part
+        me = lax.axis_index("seq") * near + me_near
+        met = count if turns else near
 
         def place(k):
+            if not turns:
+                device = lax.rem(me_near + k, near)
+                return device, {"segment": device // parts, "mp": lax.rem(device, parts)}
             device = lax.rem(me + k, count)
             return device, {
                 "segment": lax.rem(device // parts, segments),
-                "seq": device // (parts * segments),
+                "seq": device // near,
                 "mp": lax.rem(device, parts),
             }
 
@@ -192,68 +218,123 @@
 
         @pl.when(step == 0)
         def _():
-            @pl.loop(1, count)
+            @pl.loop(1, met)
             def _(k):
                 pl.semaphore_signal(
                     barrier, inc=1, device_id=place(k)[1], device_id_type=pl.DeviceIdType.MESH
                 )
 
-        kernel(*refs[: n_in + n_out], Outgoing(slots, step))
+        kernel(
+            *ins,
+            *([Handed(held, step)] if hands else []),
+            *local,
+            *([Outgoing(slots, step)] if turns else []),
+        )
 
         @pl.when(step == group - 1)
         def _():
-            pl.semaphore_wait(barrier, count - 1)
+            pl.semaphore_wait(barrier, met - 1)
 
         @pl.when(lax.rem(step, group) == group - 1)
         def _():
             base = step - (group - 1)
-            target = got.at[pl.ds(me * own + base, group)]
-
-            @pl.loop(1, count)
-            def _(k):
-                device, where = place(k)
-                pltpu.make_async_remote_copy(
-                    src_ref=slots.at[device, pl.ds(base, group)],
-                    dst_ref=target,
-                    send_sem=send_sem,
-                    recv_sem=recv_sem,
-                    device_id=where,
-                    device_id_type=pl.DeviceIdType.MESH,
-                ).start()
+            if turns:
+                target = got.at[pl.ds(me * own + base, group)]
+
+                @pl.loop(1, count)
+                def _(k):
+                    device, where = place(k)
+                    pltpu.make_async_remote_copy(
+                        src_ref=slots.at[device, pl.ds(base, group)],
+                        dst_ref=target,
+                        send_sem=send_sem,
+                        recv_sem=recv_sem,
+                        device_id=where,
+                        device_id_type=pl.DeviceIdType.MESH,
+                    ).start()
+
+            if hands:
+                for h in range(parts):
+
+                    @pl.when(me_near != layer * parts + h)
+                    def _():
+                        pltpu.make_async_remote_copy(
+                            src_ref=held.at[pl.ds(base, group), pl.ds(h * half, half)],
+                            dst_ref=grads.at[me_near, pl.ds(base, group)],
+                            send_sem=grad_send,
+                            recv_sem=grad_recv,
+                            device_id={"segment": layer, "mp": h},
+                            device_id_type=pl.DeviceIdType.MESH,
+                        ).start()
 
         @pl.when(step == own - 1)
         def _():
-            mine = pltpu.make_async_copy(slots.at[me], got.at[pl.ds(me * own, own)], own_sem)
-            mine.start()
-            mine.wait()
-            others = slots.at[pl.ds(0, count - 1)]
-            pltpu.make_async_copy(others, others, send_sem).wait()
-            arrived = got.at[pl.ds(0, (count - 1) * own)]
-            pltpu.make_async_copy(arrived, arrived, recv_sem).wait()
-
+            if hands:
+                for h in range(parts):
+
+                    @pl.when(me_near == layer * parts + h)
+                    def _():
+                        mine = pltpu.make_async_copy(
+                            held.at[:, pl.ds(h * half, half)], grads.at[layer * parts + h], grad_own
+                        )
+                        mine.start()
+                        mine.wait()
+
+            if turns:
+                mine = pltpu.make_async_copy(slots.at[me], got.at[pl.ds(me * own, own)], own_sem)
+                mine.start()
+                mine.wait()
+                others = slots.at[pl.ds(0, count - 1)]
+                pltpu.make_async_copy(others, others, send_sem).wait()
+                arrived = got.at[pl.ds(0, (count - 1) * own)]
+                pltpu.make_async_copy(arrived, arrived, recv_sem).wait()
+            if hands:
+
+                @pl.when(segment == layer)
+                def _():
+                    if parts > 1:
+                        some = held.at[:, pl.ds(0, (parts - 1) * half)]
+                        pltpu.make_async_copy(some, some, grad_send).wait()
+                    arrived = grads.at[pl.ds(0, near - 1)]
+                    pltpu.make_async_copy(arrived, arrived, grad_recv).wait()
+
+                @pl.when(segment != layer)
+                def _():
+                    pltpu.make_async_copy(held, held, grad_send).wait()
+
+    any_place = pl.BlockSpec(memory_space=pl.ANY)
+    specs = [blocked(s) for s, _ in outs]
+    shapes = [jax.ShapeDtypeStruct(s, d) for s, d in outs]
+    scratch = []
+    if turns:
+        specs.append(any_place)
+        shapes.append(jax.ShapeDtypeStruct((count * own, own, channels), BF))
+        scratch += [pltpu.VMEM((count, own, own, channels), BF)] + [pltpu.SemaphoreType.DMA] * 3
+    if hands:
+        specs.append(any_place)
+        shapes.append(jax.ShapeDtypeStruct((near, own, half, size), BF))
+        scratch += [pltpu.VMEM((own, size, size), BF)] + [pltpu.SemaphoreType.DMA] * 3
     moved = sum(a.size * a.dtype.itemsize for a, _ in operands)
-    result = pl.pallas_call(
-        body,
-        grid=(steps,),
-        in_specs=[spec(a.shape, how) for a, how in operands],
-        out_specs=[blocked(s) for s, _ in outs] + [pl.BlockSpec(memory_space=pl.ANY)],
-        out_shape=[jax.ShapeDtypeStruct(s, d) for s, d in outs]
-        + [jax.ShapeDtypeStruct((count * own, own, channels), BF)],
-        scratch_shapes=[
-            pltpu.VMEM((count, own, own, channels), BF),
-            pltpu.SemaphoreType.DMA,
-            pltpu.SemaphoreType.DMA,
-            pltpu.SemaphoreType.DMA,
-        ],
-        cost_estimate=pl.CostEstimate(
-            flops=flops, bytes_accessed=moved + 150_000_000, transcendentals=0
-        ),
-        compiler_params=pltpu.CompilerParams(
-            vmem_limit_bytes=VMEM_LIMIT, dimension_semantics=("arbitrary",),
-            collective_id=collective_id, has_side_effects=True,
-        ),
-    )(*[a for a, _ in operands])
-    return list(result[:-1]) + [jnp.swapaxes(result[-1], 0, 1)]
+    result = list(
+        pl.pallas_call(
+            body,
+            grid=(steps,),
+            in_specs=[spec(a.shape, how) for a, how in operands],
+            out_specs=specs,
+            out_shape=shapes,
+            scratch_shapes=scratch,
+            cost_estimate=pl.CostEstimate(
+                flops=flops, bytes_accessed=moved + 150_000_000, transcendentals=0
+            ),
+            compiler_params=pltpu.CompilerParams(
+                vmem_limit_bytes=VMEM_LIMIT, dimension_semantics=("arbitrary",),
+                collective_id=collective_id, has_side_effects=True,
+            ),
+        )(*[a for a, _ in operands])
+    )
+    if turns:
+        result[n_out] = jnp.swapaxes(result[n_out], 0, 1)
+    return result
 
 
 def order_columns(rows):
@@ -376,10 +457,6 @@
     cube = 2 * own * size * size * model
     feed = 2 * own * size * model * (2 * model + 2 * hidden)
 
-    def halves(grad):
-        cut = grad.reshape(own, parts, size // parts, size)
-        return jnp.stack(swap([cut[:, n] for n in range(parts)], "mp"))
-
     key_low = lax.dynamic_slice_in_dim(keys[0], part * channels, channels, 1)
     (mixed_low,) = run(
         rows_kernel, core_rows,
@@ -390,57 +467,54 @@
     mixed_low, in_cols = lax.optimization_barrier((order_columns(mixed_low), in_cols))
     mixed_low = turn_split(mixed_low)
     cot_cols = turn_split(order_columns(core_cot))
-    middle, middle_rows = run_and_turn(
+    middle, middle_rows = run_and_send(
         forward_kernel, own,
-        [(mixed_low, True), (second_low_block, True), (in_cols, True), (gates[0], False)] + ffn(0),
-        [(grid_rows, BF)], cube + feed, model, 0,
+        [(second_low_block, True), (mixed_low, True), (in_cols, True), (gates[0], False)] + ffn(0),
+        [(grid_rows, BF)], cube + feed, 0, channels=model,
     )
     middle_rows, cot_cols = lax.optimization_barrier((middle_rows, cot_cols))
-    (mixed_high,) = run_and_turn(
+    (mixed_high,) = run_and_send(
         rows_kernel, own,
         [(middle_rows, True), (keys[1], False), (first_high, True)],
-        [], cube, model, 1,
-    )
-    second_high, direct, back_rows = run_and_turn(
+        [], cube, 1, channels=model, group=2,
+    )
+    direct, back_rows, second_high = run_and_send(
         upper_kernel, own,
         [
-            (cot_cols, True), (mixed_high, True), (second_high_block, True),
+            (second_high_block, True), (cot_cols, True), (mixed_high, True),
             (middle, True), (gates[1], False),
         ] + ffn(1),
-        [(grad_shape, BF), (grid_rows, F32)], 3 * cube + 2 * feed, model, 2,
-    )
-    grad_high, scaled_cols = run_and_turn(
+        [(grid_rows, F32)], 3 * cube + 2 * feed, 2, channels=model, layer=1,
+    )
+    scaled_cols, grad_high = run_and_send(
         rows_back_kernel, own,
         [(back_rows, True), (middle_rows, True), (keys[1], False), (first_high, True)],
-        [(grad_shape, BF)], 2 * cube, model, 3,
+        [], 2 * cube, 3, channels=model, layer=1, group=2,
     )
     in_cut = core_in.reshape(parts, own, size, channels)
     in_rows = jnp.concatenate(swap([in_cut[n] for n in range(parts)], "mp"), axis=2)
-    second_high = halves(second_high)
-    scaled_cols, in_rows, second_high = lax.optimization_barrier(
-        (scaled_cols, in_rows, second_high)
-    )
-    grad_high = halves(grad_high)
-    second_low, low_rows = run_and_turn(
+    scaled_cols, in_rows = lax.optimization_barrier((scaled_cols, in_rows))
+    low_rows, second_low = run_and_send(
         lower_kernel, own,
         [
-            (direct, True), (scaled_cols, True), (keys[1], False), (mixed_low, True),
-            (second_low_block, True), (in_cols, True), (gates[0], False),
+            (direct, True), (scaled_cols, True), (keys[1], False), (second_low_block, True),
+            (mixed_low, True), (in_cols, True), (gates[0], False),
         ] + ffn(0),
-        [(grad_shape, BF)], 3 * cube + 2 * feed, model, 4,
-    )
-    low_rows, grad_high = lax.optimization_barrier((low_rows, grad_high))
-    (grad_low,) = run(
+        [], 3 * cube + 2 * feed, 4, channels=model, layer=0,
+    )
+
+    def result(low, high):
+        chosen = jnp.where(segment == 0, low, high)
+        return chosen.reshape(1, held, size // parts, size).astype(F32)
+
+    second_out = result(second_low, second_high)
+    low_rows, second_out = lax.optimization_barrier((low_rows, second_out))
+    (grad_low,) = run_and_send(
         rows_grad_kernel, own,
         [(low_rows, True), (in_rows, True), (keys[0], False)],
-        [(grad_shape, BF)], cube,
-    )
-
-    def hand_out(low, high):
-        got = jnp.stack(swap([halves(low), high], "segment"))
-        return got.reshape(1, held, size // parts, size).astype(F32)
-
-    return hand_out(grad_low, grad_high), hand_out(second_low, second_high)
+        [], cube, 5, layer=0, group=2,
+    )
+    return result(grad_low, grad_high), second_out
 
 
 def solution(mesh):

time: 483 us -> 497 us (1.029)
  waiting for transfers between devices: 80.8 us -> 103 us
  starting transfers between devices: 22.7 us -> 16.9 us
    ppermute x9 -> x3, waiting for transfers between devices: 19 us -> 41.4 us  [swap(): held.append(lax.ppermute(chosen((me + shift) % count), axis, route))]
    ppermute x9 -> x3, starting transfers between devices: 7.61 us -> 1.77 us  [swap(): held.append(lax.ppermute(chosen((me + shift) % count), axis, route))]
    pallas_call x2 -> x1, Pallas kernels: 11.3 us -> 9.14 us  [run(): pl.pallas_call(kernel, grid=(steps,), in_specs=[spec(a.shape, how) for a,...]
    pallas_call x5 -> x6, Pallas kernels: 274 us -> 273 us  [run_and_send(): pl.pallas_call(body, grid=(steps,), in_specs=[spec(a.shape, how) for a, h...]
    unnamed x58 -> x60, local copies, waits for them, and re-layouts: 11.7 us -> 11.8 us
  transfers between devices with their start and end apart: 13 -> 7, of which waited for: 4 -> 3; matrix products, arithmetic and copies ran while one was open for 10% -> 7% of each run, Pallas kernels for 59% -> 12%
where the time goes in v4:
time: 497 us; the launch traced here: 495 us
  Pallas kernels  282 us (57%)
  waiting for transfers between devices  103 us (21%)
  local copies, waits for them, and re-layouts  42.2 us (8%)
  other arithmetic  23.3 us (5%)
  starting transfers between devices  16.9 us (3%)
  between operations  14.6 us (3%)
  blocking collectives  11.6 us (2%)
    pallas_call x6, Pallas kernels, run_and_send(): pl.pallas_call(body, grid=(steps,), in_specs=[spec(a.shape, how) for a, h...  273 us
    all_to_all x3, waiting for transfers between devices, turn_split(): got = lax.all_to_all(sent, ALL, split_axis=0, concat_axis=0, tiled=True)  61.8 us
    ppermute x3, waiting for transfers between devices, swap(): held.append(lax.ppermute(chosen((me + shift) % count), axis, route))  41.4 us
    all_to_all x3, starting transfers between devices, turn_split(): got = lax.all_to_all(sent, ALL, split_axis=0, concat_axis=0, tiled=True)  15 us
    unnamed x60, local copies, waits for them, and re-layouts  11.8 us
    all_gather x1, blocking collectives, on_device(): gains = lax.all_gather(gains, ('segment', 'mp'), axis=0, tiled=False)  11.6 us
    pallas_call x5, local copies, waits for them, and re-layouts, run_and_send(): pl.pallas_call(body, grid=(steps,), in_specs=[spec(a.shape, how) for a, h...  10.6 us
  transfers between devices with their start and end apart: 7, of which 3 were waited for; matrix products, arithmetic and copies ran while one was open for 7% of the time, Pallas kernels for 12%

profile of v4, /device:TPU:0, one launch (start us, length us, event | category | flops | bytes accessed | tf_op | source)
XLA Modules:
  0.0 495.3 jit_solution(8166564129661839184)
XLA Ops:
  7.2 1.7 fusion.9
  8.9 2.5 copy.27
  11.4 7.4 %all-to-all-start = ((bf16[256,16,256]{2,1,0:T(8,128)(2,1)}), bf16[256,16,256]{2,1,0:T(8,128)(2,1)}, u32[]{:S(2)}, u32[]{:S(2)}) async-start(bf16[256,16,256]{2,1,0:T(8,128)(2,1)} %copy.27), calls=%async_computation | async-start | bytes 4194304 | tf_op jit(solution)/shard_map/all_to_all | solution.py:348
  18.9 3.8 select_bitcast_fusion.1
  22.9 11.6 %all-gather.2 = f32[4,2,256]{2,1,0:T(2,128)S(1)} all-gather(f32[1,2,256]{2,1,0:T(2,128)S(1)} %maximum_bitcast_fusion), channel_id=2, replica_groups=mesh['segment'=2,'seq'=8,'mp'=2] {'segment','mp'}, dimensions={0}, use_global_device_ids=true | all-gather | bytes 10240 | tf_op jit(solution)/shard_map/all_gather | solution.py:410
  34.5 1.9 constant_dynamic-slice_fusion.2.x_ref
  37.3 2.5 broadcast_select_fusion
  39.9 9.1 %shard_map.113 = bf16[16,256,256]{2,1,0:T(8,128)(2,1)S(1)} custom-call(bf16[16,256,256]{2,1,0:T(8,128)(2,1)S(1)} %constant_dynamic-slice_fusion.2.x_ref, f32[1,256]{1,0:T(1,128)S(1)} %constant_dynamic-slice_fusion.1.key_ref, bf16[16,256,256]{2,1,0:T(8,128)(2,1)} %get-tuple-element.36.first_ref), custom_call_target="tpu_custom_call" | custom-call | flops 536870912 | bytes 6292480 | tf_op jit(solution)/shard_map/pallas_call | solution.py:147
  49.1 18.5 %all-to-all-done = bf16[256,16,256]{2,1,0:T(8,128)(2,1)} async-done(((bf16[256,16,256]{2,1,0:T(8,128)(2,1)}), bf16[256,16,256]{2,1,0:T(8,128)(2,1)}, u32[]{:S(2)}, u32[]{:S(2)}) %all-to-all-start) | async-done | bytes 2097184 | tf_op jit(solution)/shard_map/all_to_all | solution.py:348
  67.6 2.6 copy.28
  70.2 3.7 all-to-all-start.1
  75.0 1.7 constant_dynamic-slice_fusion
  76.8 2.5 copy.58
  79.3 43.3 %all-to-all-done.1 = bf16[256,16,256]{2,1,0:T(8,128)(2,1)S(1)} async-done(((bf16[256,16,256]{2,1,0:T(8,128)(2,1)}), bf16[256,16,256]{2,1,0:T(8,128)(2,1)S(1)}, u32[]{:S(2)}, u32[]{:S(2)}) %all-to-all-start.1) | async-done | bytes 2097184 | tf_op jit(solution)/shard_map/all_to_all | solution.py:348
  123.9 4.0 all-to-all-start.2
  127.8 2.7 broadcast_select_fusion.5
  133.9 41.4 %collective-permute-done.2 = bf16[8,256,256]{2,1,0:T(8,128)(2,1)S(1)} collective-permute-done((bf16[8,256,256]{2,1,0:T(8,128)(2,1)}, bf16[8,256,256]{2,1,0:T(8,128)(2,1)S(1)}, u32[]{:S(2)}, u32[]{:S(2)}) %collective-permute-start.2) | collective-permute-done | bytes 1048608 | tf_op jit(solution)/shard_map/ppermute | solution.py:370
  175.3 1.7 broadcast_select_fusion.6
  190.3 2.5 reshape.109.refs_5_.refs_6_.refs_8_
  196.4 51.3 %shard_map.114 = (bf16[8,256,512]{2,1,0:T(8,128)(2,1)}, bf16[256,8,512]{2,1,0:T(8,128)(2,1)}) custom-call(bf16[8,256,256]{2,1,0:T(8,128)(2,1)S(1)} %get-tuple-element.40.refs_0_.refs_3_, bf16[16,2,8,16,256]{4,3,2,1,0:T(8,128)(2,1)} %bitcast.112, bf16[16,2,8,16,256]{4,3,2,1,0:T(8,128)(2,1)} %bitcast.11.refs_2_.refs_5_, f32[1,512]{1,0:T(1,128)S(1)} %bitcast.98, ...), custom_call_target="tpu_custom_call" | custom-call | flops 4831838208 | bytes 159439232 | tf_op jit(solution)/shard_map/pallas_call | solution.py:319
  247.8 2.3 copy.63
  250.1 48.4 %shard_map.115 = bf16[256,8,512]{2,1,0:T(8,128)(2,1)S(1)} custom-call(bf16[8,256,512]{2,1,0:T(8,128)(2,1)S(1)} %bitcast.86, f32[1,512]{1,0:T(1,128)S(1)} %bitcast.93, bf16[8,256,256]{2,1,0:T(8,128)(2,1)S(1)} %dynamic-slice_select_fusion.refs_2_.refs_3_), custom_call_target="tpu_custom_call" | custom-call | flops 536870912 | bytes 153147776 | tf_op jit(solution)/shard_map/pallas_call | solution.py:319
  298.5 2.0 copy.62
  301.4 54.8 %shard_map.116 = (f32[8,256,512]{2,1,0:T(8,128)}, bf16[256,8,512]{2,1,0:T(8,128)(2,1)}, bf16[4,8,128,256]{3,2,1,0:T(8,128)(2,1)}) custom-call(bf16[8,256,256]{2,1,0:T(8,128)(2,1)S(1)} %copy-done.3, bf16[16,2,8,16,256]{4,3,2,1,0:T(8,128)(2,1)} %bitcast.26.refs_1_, bf16[8,256,512]{2,1,0:T(8,128)(2,1)} %bitcast.115, ...), custom_call_target="tpu_custom_call" | custom-call | flops 10200547328 | bytes 161536384 | tf_op jit(solution)/shard_map/pallas_call | solution.py:319
  356.2 3.6 copy.61
  359.8 48.7 %shard_map.117 = (bf16[256,8,512]{2,1,0:T(8,128)(2,1)S(1)}, bf16[4,8,128,256]{3,2,1,0:T(8,128)(2,1)S(1)}) custom-call(bf16[8,256,512]{2,1,0:T(8,128)(2,1)} %bitcast.107, bf16[8,256,512]{2,1,0:T(8,128)(2,1)} %bitcast.87, f32[1,512]{1,0:T(1,128)S(1)} %bitcast.94, bf16[8,256,256]{2,1,0:T(8,128)(2,1)S(1)} %dynamic-slice_select_fusion.refs_2_.refs_3_), custom_call_target="tpu_custom_call" | custom-call | flops 1073741824 | bytes 155244928 | tf_op jit(solution)/shard_map/pallas_call | solution.py:319
  408.5 2.0 copy.60
  410.6 54.7 %shard_map.118 = (bf16[256,8,512]{2,1,0:T(8,128)(2,1)}, bf16[4,8,128,256]{3,2,1,0:T(8,128)(2,1)}) custom-call(f32[8,256,512]{2,1,0:T(8,128)} %get-tuple-element.25.refs_0_, bf16[8,256,512]{2,1,0:T(8,128)(2,1)} %bitcast.114, f32[1,512]{1,0:T(1,128)S(1)} %bitcast.95, bf16[8,256,256]{2,1,0:T(8,128)(2,1)S(1)} %copy-done.2, ...), custom_call_target="tpu_custom_call" | custom-call | flops 10200547328 | bytes 165732736 | tf_op jit(solution)/shard_map/pallas_call | solution.py:319
  465.3 1.9 broadcast_select_fusion.2
  467.2 2.5 bitcast_convert_fusion.1
  470.4 15.3 %shard_map.119 = bf16[4,8,128,256]{3,2,1,0:T(8,128)(2,1)S(1)} custom-call(bf16[8,256,512]{2,1,0:T(8,128)(2,1)S(1)} %bitcast.89, bf16[8,256,512]{2,1,0:T(8,128)(2,1)} %pad_maximum_fusion.refs_1_, f32[1,512]{1,0:T(1,128)S(1)} %bitcast.97), custom_call_target="tpu_custom_call" | custom-call | flops 536870912 | bytes 154196352 | tf_op jit(solution)/shard_map/pallas_call | solution.py:319
  485.9 2.5 bitcast_convert_fusion
  (90 shorter events, 25.6 us)
Async XLA Ops:
  11.4 56.1 %all-to-all-start = ((bf16[256,16,256]{2,1,0:T(8,128)(2,1)}), bf16[256,16,256]{2,1,0:T(8,128)(2,1)}, u32[]{:S(2)}, u32[]{:S(2)}) async-start(bf16[256,16,256]{2,1,0:T(8,128)(2,1)} %copy.27), calls=%async_computation | async-start | bytes 4194304 | tf_op jit(solution)/shard_map/all_to_all | solution.py:348
  18.9 4.0 copy-start.25
  18.9 4.0 copy-start.26
  22.7 13.8 %collective-permute-start.1 = (bf16[16,256,256]{2,1,0:T(8,128)(2,1)}, bf16[16,256,256]{2,1,0:T(8,128)(2,1)S(1)}, u32[]{:S(2)}, u32[]{:S(2)}) collective-permute-start(bf16[16,256,256]{2,1,0:T(8,128)(2,1)} %select_bitcast_fusion.1), channel_id=1, source_target_pairs={{0,16},{16,0},{1,17},{17,1},{2,18},{18,2},{3,19},{19,3},{4,20},{20... | collective-permute-start | bytes 6291464 | tf_op jit(solution)/shard_map/ppermute | solution.py:370
  34.5 2.8 copy-start.12
  37.3 2.6 copy-start.13
  70.2 3.7 copy-start.22
  70.2 3.9 copy-start.21
  70.2 3.9 copy-start.23
  70.2 3.9 copy-start.24
  70.2 52.4 %all-to-all-start.1 = ((bf16[256,16,256]{2,1,0:T(8,128)(2,1)}), bf16[256,16,256]{2,1,0:T(8,128)(2,1)S(1)}, u32[]{:S(2)}, u32[]{:S(2)}) async-start(bf16[256,16,256]{2,1,0:T(8,128)(2,1)} %copy.28), calls=%async_computation.1 | async-start | bytes 4194304 | tf_op jit(solution)/shard_map/all_to_all | solution.py:348
  73.8 107.8 %all-gather.5.cloned.1.call-start = ((), (), s32[]{:S(2)}) async-start(), calls=%async_computation.3 | async-start | bytes 3276800 | tf_op jit(solution)/shard_map/all_gather | solution.py:441
  122.6 1.3 copy-start.19
  123.9 126.2 %all-to-all-start.2 = ((bf16[256,16,256]{2,1,0:T(8,128)(2,1)}), bf16[256,16,256]{2,1,0:T(8,128)(2,1)}, u32[]{:S(2)}, u32[]{:S(2)}) async-start(bf16[256,16,256]{2,1,0:T(8,128)(2,1)} %bitcast.77), calls=%async_computation.2 | async-start | bytes 4194304 | tf_op jit(solution)/shard_map/all_to_all | solution.py:348
  130.5 44.8 %collective-permute-start.2 = (bf16[8,256,256]{2,1,0:T(8,128)(2,1)}, bf16[8,256,256]{2,1,0:T(8,128)(2,1)S(1)}, u32[]{:S(2)}, u32[]{:S(2)}) collective-permute-start(bf16[8,256,256]{2,1,0:T(8,128)(2,1)} %broadcast_select_fusion.5), channel_id=1, source_target_pairs={{0,1},{1,0},{2,3},{3,2},{4,5},{5,4},{6,7},{7,6},{8,9},{9,8},{10,11... | collective-permute-start | bytes 3145736 | tf_op jit(solution)/shard_map/ppermute | solution.py:370
  133.7 45.0 %collective-permute-start = (bf16[8,256,256]{2,1,0:T(8,128)(2,1)S(1)}, bf16[8,256,256]{2,1,0:T(8,128)(2,1)S(1)}, u32[]{:S(2)}, u32[]{:S(2)}) collective-permute-start(bf16[8,256,256]{2,1,0:T(8,128)(2,1)S(1)} %select_bitcast_fusion.2), channel_id=1, source_target_pairs={{0,16},{16,0},{1,17},{17,1},{2,18},{18,2},{3,19},{19,3},{4,20},{20... | collective-permute-start | bytes 3145736 | tf_op jit(solution)/shard_map/ppermute | solution.py:370
  177.1 2.9 copy-start.16
  178.6 2.6 copy-start.14
  178.6 2.9 copy-start.15
  181.3 11.5 %copy-start.1 = (bf16[8,256,256]{2,1,0:T(8,128)(2,1)}, bf16[8,256,256]{2,1,0:T(8,128)(2,1)S(1)}, u32[]{:S(2)}) copy-start(bf16[8,256,256]{2,1,0:T(8,128)(2,1)S(1)} %get-tuple-element.40.refs_0_.refs_3_) | copy-start | bytes 3145732
  186.3 6.5 %copy-start.4 = (bf16[2,512,512]{2,1,0:T(8,128)(2,1)}, bf16[2,512,512]{2,1,0:T(8,128)(2,1)S(1)}, u32[]{:S(2)}) copy-start(bf16[2,512,512]{2,1,0:T(8,128)(2,1)S(1)} %reshape.110.refs_7_.refs_8_.refs_10_) | copy-start | bytes 3145732
  186.3 2.5 copy-start.17
  192.8 1.2 copy-start.6
  250.0 48.4 %copy-start = (bf16[256,8,512]{2,0,1:T(8,128)(2,1)}, bf16[256,8,512]{2,0,1:T(8,128)(2,1)S(1)}, u32[]{:S(2)}) copy-start(bf16[256,8,512]{2,0,1:T(8,128)(2,1)S(1)} %copy.63) | copy-start | bytes 6291460
  250.1 50.5 %copy-start.11 = (bf16[2,4,512,128]{3,2,1,0:T(8,128)(2,1)S(1)}, bf16[2,4,512,128]{3,2,1,0:T(8,128)(2,1)}, u32[]{:S(2)}) copy-start(bf16[2,4,512,128]{3,2,1,0:T(8,128)(2,1)} %get-tuple-element.44.refs_6_.refs_7_.refs_9_) | copy-start | bytes 3145732
  298.5 2.1 copy-start.3
  298.5 2.1 copy-start.5
  298.5 2.3 copy-start.7
  298.5 2.9 copy-start.9
  408.5 2.0 copy-start.2
  410.6 54.7 %copy-start.18 = (bf16[4,8,128,256]{3,2,1,0:T(8,128)(2,1)S(1)}, bf16[4,8,128,256]{3,2,1,0:T(8,128)(2,1)}, u32[]{:S(2)}) copy-start(bf16[4,8,128,256]{3,2,1,0:T(8,128)(2,1)} %get-tuple-element.31) | copy-start | bytes 6291460
  467.2 2.5 copy-start.20
  (2 other events, 2.4 us)
Sparse Core Ops, SparseCore 0:
  76.2 35.6 all-gather.4

commit v5 on v4

--- a/solution.py
+++ b/solution.py
@@ -175,7 +175,7 @@
         self.ref[self.step] = grad
 
 
-def run_and_send(kernel, steps, operands, outs, flops, collective_id, channels=0, layer=None, group=1):
+def run_and_send(kernel, steps, operands, outs, flops, collective_id, channels=0, layer=None, group=2):
     parts, segments, seqs = lax.axis_size("mp"), lax.axis_size("segment"), lax.axis_size("seq")
     count = parts * segments * seqs
     near = parts * segments
@@ -476,8 +476,9 @@
     (mixed_high,) = run_and_send(
         rows_kernel, own,
         [(middle_rows, True), (keys[1], False), (first_high, True)],
-        [], cube, 1, channels=model, group=2,
-    )
+        [], cube, 1, channels=model,
+    )
+    mixed_high, core_late = lax.optimization_barrier((mixed_high, core_in))
     direct, back_rows, second_high = run_and_send(
         upper_kernel, own,
         [
@@ -489,9 +490,9 @@
     scaled_cols, grad_high = run_and_send(
         rows_back_kernel, own,
         [(back_rows, True), (middle_rows, True), (keys[1], False), (first_high, True)],
-        [], 2 * cube, 3, channels=model, layer=1, group=2,
-    )
-    in_cut = core_in.reshape(parts, own, size, channels)
+        [], 2 * cube, 3, channels=model, layer=1,
+    )
+    in_cut = core_late.reshape(parts, own, size, channels)
     in_rows = jnp.concatenate(swap([in_cut[n] for n in range(parts)], "mp"), axis=2)
     scaled_cols, in_rows = lax.optimization_barrier((scaled_cols, in_rows))
     low_rows, second_low = run_and_send(
@@ -512,7 +513,7 @@
     (grad_low,) = run_and_send(
         rows_grad_kernel, own,
         [(low_rows, True), (in_rows, True), (keys[0], False)],
-        [], cube, 5, layer=0, group=2,
+        [], cube, 5, layer=0,
     )
     return result(grad_low, grad_high), second_out
 

time: 497 us -> 480 us (0.966)
  waiting for transfers between devices: 103 us -> 63.5 us
  Pallas kernels: 282 us -> 297 us
  local copies, waits for them, and re-layouts: 42.2 us -> 48.1 us
    ppermute x3, waiting for transfers between devices: 41.4 us -> 2.76 us  [swap(): held.append(lax.ppermute(chosen((me + shift) % count), axis, route))]
    pallas_call x6, Pallas kernels: 273 us -> 288 us  [run_and_send(): pl.pallas_call(body, grid=(steps,), in_specs=[spec(a.shape, how) for a, h...]
    unnamed x60 -> x54, local copies, waits for them, and re-layouts: 11.8 us -> 13.2 us
  transfers between devices with their start and end apart: 7 -> 7, of which waited for: 3 -> 3; matrix products, arithmetic and copies ran while one was open for 7% -> 9% of each run, Pallas kernels for 12% -> 38%
where the time goes in v5:
time: 480 us; the launch traced here: 476 us
  Pallas kernels  297 us (62%)
  waiting for transfers between devices  63.5 us (13%)
  local copies, waits for them, and re-layouts  48.1 us (10%)
  other arithmetic  23.1 us (5%)
  starting transfers between devices  16.5 us (3%)
  between operations  14.4 us (3%)
  blocking collectives  11.6 us (2%)
    pallas_call x6, Pallas kernels, run_and_send(): pl.pallas_call(body, grid=(steps,), in_specs=[spec(a.shape, how) for a, h...  288 us
    all_to_all x3, waiting for transfers between devices, turn_split(): got = lax.all_to_all(sent, ALL, split_axis=0, concat_axis=0, tiled=True)  60.7 us
    all_to_all x3, starting transfers between devices, turn_split(): got = lax.all_to_all(sent, ALL, split_axis=0, concat_axis=0, tiled=True)  15.2 us
    unnamed x54, local copies, waits for them, and re-layouts  13.2 us
    pallas_call x5, local copies, waits for them, and re-layouts, run_and_send(): pl.pallas_call(body, grid=(steps,), in_specs=[spec(a.shape, how) for a, h...  11.9 us
    all_gather x1, blocking collectives, on_device(): gains = lax.all_gather(gains, ('segment', 'mp'), axis=0, tiled=False)  11.6 us
  transfers between devices with their start and end apart: 7, of which 3 were waited for; matrix products, arithmetic and copies ran while one was open for 9% of the time, Pallas kernels for 38%

profile of v5, /device:TPU:0, one launch (start us, length us, event | category | flops | bytes accessed | tf_op | source)
XLA Modules:
  0.0 476.2 jit_solution(9966925378860233193)
XLA Ops:
  9.0 2.5 copy.27
  11.5 7.4 %all-to-all-start = ((bf16[256,16,256]{2,1,0:T(8,128)(2,1)}), bf16[256,16,256]{2,1,0:T(8,128)(2,1)}, u32[]{:S(2)}, u32[]{:S(2)}) async-start(bf16[256,16,256]{2,1,0:T(8,128)(2,1)} %copy.27), calls=%async_computation | async-start | bytes 4194304 | tf_op jit(solution)/shard_map/all_to_all | solution.py:348
  18.9 3.8 select_bitcast_fusion.1
  22.9 11.6 %all-gather.2 = f32[4,2,256]{2,1,0:T(2,128)S(1)} all-gather(f32[1,2,256]{2,1,0:T(2,128)S(1)} %maximum_bitcast_fusion), channel_id=2, replica_groups=mesh['segment'=2,'seq'=8,'mp'=2] {'segment','mp'}, dimensions={0}, use_global_device_ids=true | all-gather | bytes 10240 | tf_op jit(solution)/shard_map/all_gather | solution.py:410
  34.5 1.9 constant_dynamic-slice_fusion.2.x_ref
  37.3 2.4 broadcast_select_fusion
  39.7 9.1 %shard_map.113 = bf16[16,256,256]{2,1,0:T(8,128)(2,1)S(1)} custom-call(bf16[16,256,256]{2,1,0:T(8,128)(2,1)S(1)} %constant_dynamic-slice_fusion.2.x_ref, f32[1,256]{1,0:T(1,128)S(1)} %constant_dynamic-slice_fusion.1.key_ref, bf16[16,256,256]{2,1,0:T(8,128)(2,1)} %get-tuple-element.40.first_ref), custom_call_target="tpu_custom_call" | custom-call | flops 536870912 | bytes 6292480 | tf_op jit(solution)/shard_map/pallas_call | solution.py:147
  50.2 17.4 %all-to-all-done = bf16[256,16,256]{2,1,0:T(8,128)(2,1)} async-done(((bf16[256,16,256]{2,1,0:T(8,128)(2,1)}), bf16[256,16,256]{2,1,0:T(8,128)(2,1)}, u32[]{:S(2)}, u32[]{:S(2)}) %all-to-all-start) | async-done | bytes 2097184 | tf_op jit(solution)/shard_map/all_to_all | solution.py:348
  67.6 4.1 copy.28
  71.7 3.8 all-to-all-start.1
  78.4 2.5 copy.58
  80.9 43.3 %all-to-all-done.1 = bf16[256,16,256]{2,1,0:T(8,128)(2,1)} async-done(((bf16[256,16,256]{2,1,0:T(8,128)(2,1)}), bf16[256,16,256]{2,1,0:T(8,128)(2,1)}, u32[]{:S(2)}, u32[]{:S(2)}) %all-to-all-start.1) | async-done | bytes 2097184 | tf_op jit(solution)/shard_map/all_to_all | solution.py:348
  124.2 4.0 all-to-all-start.2
  128.2 2.7 select_bitcast_fusion.2
  130.9 2.8 collective-permute-done
  133.7 3.1 bitcast_select_fusion
  140.8 2.4 copy.32
  143.2 2.2 reshape.110.refs_7_.refs_8_.refs_10_
  148.8 2.5 reshape.109.refs_5_.refs_6_.refs_8_
  157.4 62.1 %shard_map.114 = (bf16[8,256,512]{2,1,0:T(8,128)(2,1)}, bf16[256,8,512]{2,1,0:T(8,128)(2,1)}) custom-call(bf16[8,256,256]{2,1,0:T(8,128)(2,1)S(1)} %copy-done.2, bf16[16,2,8,16,256]{4,3,2,1,0:T(8,128)(2,1)} %bitcast.12.refs_1_.refs_4_, bf16[16,2,8,16,256]{4,3,2,1,0:T(8,128)(2,1)} %bitcast.11.refs_2_.refs_5_, f32[1,512]{1,0:T(1,128)S(1)} %bitcast.98, ...), custom_call_target="tpu_custom_call" | custom-call | flops 4831838208 | bytes 159439232 | tf_op jit(solution)/shard_map/pallas_call | solution.py:319
  219.5 3.6 copy.63
  224.7 48.8 %shard_map.115 = bf16[256,8,512]{2,1,0:T(8,128)(2,1)S(1)} custom-call(bf16[8,256,512]{2,1,0:T(8,128)(2,1)S(1)} %bitcast.87, f32[1,512]{1,0:T(1,128)S(1)} %bitcast.93, bf16[8,256,256]{2,1,0:T(8,128)(2,1)S(1)} %dynamic-slice_select_fusion.refs_2_.refs_3_), custom_call_target="tpu_custom_call" | custom-call | flops 536870912 | bytes 153147776 | tf_op jit(solution)/shard_map/pallas_call | solution.py:319
  273.6 2.0 copy.62
  277.5 57.0 %shard_map.116 = (f32[8,256,512]{2,1,0:T(8,128)}, bf16[256,8,512]{2,1,0:T(8,128)(2,1)}, bf16[4,8,128,256]{3,2,1,0:T(8,128)(2,1)}) custom-call(bf16[8,256,256]{2,1,0:T(8,128)(2,1)S(1)} %copy-done.4, bf16[16,2,8,16,256]{4,3,2,1,0:T(8,128)(2,1)} %bitcast.26.refs_1_, bf16[8,256,512]{2,1,0:T(8,128)(2,1)} %bitcast.112, ...), custom_call_target="tpu_custom_call" | custom-call | flops 10200547328 | bytes 161536384 | tf_op jit(solution)/shard_map/pallas_call | solution.py:319
  334.5 3.6 copy.61
  338.0 51.6 %shard_map.117 = (bf16[256,8,512]{2,1,0:T(8,128)(2,1)S(1)}, bf16[4,8,128,256]{3,2,1,0:T(8,128)(2,1)S(1)}) custom-call(bf16[8,256,512]{2,1,0:T(8,128)(2,1)} %bitcast.103, bf16[8,256,512]{2,1,0:T(8,128)(2,1)} %bitcast.86, f32[1,512]{1,0:T(1,128)S(1)} %bitcast.94, bf16[8,256,256]{2,1,0:T(8,128)(2,1)S(1)} %dynamic-slice_select_fusion.refs_2_.refs_3_), custom_call_target="tpu_custom_call" | custom-call | flops 1073741824 | bytes 155244928 | tf_op jit(solution)/shard_map/pallas_call | solution.py:319
  389.6 2.0 copy.60
  393.3 52.8 %shard_map.118 = (bf16[256,8,512]{2,1,0:T(8,128)(2,1)}, bf16[4,8,128,256]{3,2,1,0:T(8,128)(2,1)}) custom-call(f32[8,256,512]{2,1,0:T(8,128)} %get-tuple-element.28.refs_0_, bf16[8,256,512]{2,1,0:T(8,128)(2,1)} %bitcast.111, f32[1,512]{1,0:T(1,128)S(1)} %bitcast.95, bf16[8,256,256]{2,1,0:T(8,128)(2,1)S(1)} %copy-done.3, ...), custom_call_target="tpu_custom_call" | custom-call | flops 10200547328 | bytes 165732736 | tf_op jit(solution)/shard_map/pallas_call | solution.py:319
  446.2 1.9 broadcast_select_fusion.2
  448.1 2.5 bitcast_convert_fusion.1
  451.4 15.3 %shard_map.119 = bf16[4,8,128,256]{3,2,1,0:T(8,128)(2,1)S(1)} custom-call(bf16[8,256,512]{2,1,0:T(8,128)(2,1)S(1)} %bitcast.89, bf16[8,256,512]{2,1,0:T(8,128)(2,1)} %pad_maximum_fusion.refs_1_, f32[1,512]{1,0:T(1,128)S(1)} %bitcast.97), custom_call_target="tpu_custom_call" | custom-call | flops 536870912 | bytes 154196352 | tf_op jit(solution)/shard_map/pallas_call | solution.py:319
  466.9 2.5 bitcast_convert_fusion
  (84 shorter events, 26.6 us)
Async XLA Ops:
  11.5 56.1 %all-to-all-start = ((bf16[256,16,256]{2,1,0:T(8,128)(2,1)}), bf16[256,16,256]{2,1,0:T(8,128)(2,1)}, u32[]{:S(2)}, u32[]{:S(2)}) async-start(bf16[256,16,256]{2,1,0:T(8,128)(2,1)} %copy.27), calls=%async_computation | async-start | bytes 4194304 | tf_op jit(solution)/shard_map/all_to_all | solution.py:348
  18.9 4.0 copy-start.22
  18.9 4.0 copy-start.23
  22.7 13.8 %collective-permute-start.1 = (bf16[16,256,256]{2,1,0:T(8,128)(2,1)}, bf16[16,256,256]{2,1,0:T(8,128)(2,1)}, u32[]{:S(2)}, u32[]{:S(2)}) collective-permute-start(bf16[16,256,256]{2,1,0:T(8,128)(2,1)} %select_bitcast_fusion.1), channel_id=1, source_target_pairs={{0,16},{16,0},{1,17},{17,1},{2,18},{18,2},{3,19},{19,3},{4,20},{20... | collective-permute-start | bytes 6291464 | tf_op jit(solution)/shard_map/ppermute | solution.py:370
  34.5 2.8 copy-start.13
  48.8 1.3 copy-start.1
  71.7 3.9 copy-start.19
  71.7 4.0 copy-start.18
  71.7 4.0 copy-start.20
  71.7 4.0 copy-start.21
  71.7 52.5 %all-to-all-start.1 = ((bf16[256,16,256]{2,1,0:T(8,128)(2,1)}), bf16[256,16,256]{2,1,0:T(8,128)(2,1)}, u32[]{:S(2)}, u32[]{:S(2)}) async-start(bf16[256,16,256]{2,1,0:T(8,128)(2,1)} %copy.28), calls=%async_computation.1 | async-start | bytes 4194304 | tf_op jit(solution)/shard_map/all_to_all | solution.py:348
  75.5 62.6 %all-gather.5.cloned.1.call-start = ((), (), s32[]{:S(2)}) async-start(), calls=%async_computation.3 | async-start | bytes 3276800 | tf_op jit(solution)/shard_map/all_gather | solution.py:441
  124.2 98.9 %all-to-all-start.2 = ((bf16[256,16,256]{2,1,0:T(8,128)(2,1)}), bf16[256,16,256]{2,1,0:T(8,128)(2,1)}, u32[]{:S(2)}, u32[]{:S(2)}) async-start(bf16[256,16,256]{2,1,0:T(8,128)(2,1)} %bitcast.104), calls=%async_computation.2 | async-start | bytes 4194304 | tf_op jit(solution)/shard_map/all_to_all | solution.py:348
  130.8 2.9 collective-permute-start
  130.9 5.9 %copy-start.14 = (bf16[16,256,256]{2,1,0:T(8,128)(2,1)S(1)}, bf16[16,256,256]{2,1,0:T(8,128)(2,1)}, u32[]{:S(2)}) copy-start(bf16[16,256,256]{2,1,0:T(8,128)(2,1)} %get-tuple-element.41) | copy-start | bytes 6291460
  145.5 1.9 copy-start.15
  151.3 1.2 copy-start.2
  152.5 1.2 copy-start.5
  153.7 1.2 copy-start.7
  155.0 1.2 copy-start.9
  156.2 1.2 copy-start.11
  223.1 1.6 copy-start
  273.5 3.3 copy-start.10
  273.6 3.3 copy-start.12
  275.6 1.3 copy-start.4
  275.6 1.5 copy-start.6
  275.6 1.9 copy-start.8
  275.7 115.9 %collective-permute-start.2 = (bf16[8,256,256]{2,1,0:T(8,128)(2,1)S(1)}, bf16[8,256,256]{2,1,0:T(8,128)(2,1)S(1)}, u32[]{:S(2)}, u32[]{:S(2)}) collective-permute-start(bf16[8,256,256]{2,1,0:T(8,128)(2,1)S(1)} %broadcast_select_fusion.5), channel_id=1, source_target_pairs={{0,1},{1,0},{2,3},{3,2},{4,5},{5,4},{6,7},{7,6},{8,9},{9,8},{10,11... | collective-permute-start | bytes 3145736 | tf_op jit(solution)/shard_map/ppermute | solution.py:370
  391.8 1.5 copy-start.3
  393.3 52.8 %copy-start.16 = (bf16[4,8,128,256]{3,2,1,0:T(8,128)(2,1)S(1)}, bf16[4,8,128,256]{3,2,1,0:T(8,128)(2,1)}, u32[]{:S(2)}) copy-start(bf16[4,8,128,256]{3,2,1,0:T(8,128)(2,1)} %get-tuple-element.35) | copy-start | bytes 6291460
  448.1 2.5 copy-start.17
Sparse Core Ops, SparseCore 0:
  77.9 35.6 all-gather.4
